TPU v7x, 32 devices: a whole 2x2x4 slice. The times are simulated.
32 devices in a mesh: groups: 2 (over x), rows: 16 (over z, y, core).
Axes of the slice: x: 2, y: 2, z: 4, core: 2. Of those that a mesh axis runs over, the one named last changes fastest.
Arguments:
- pixels: bfloat16 [128, 16, 512], P(('groups', 'rows')), parts along dimension 0, may hold values from -6 to 6
- weight_first: bfloat16 [3, 3, 512, 512], replicated, may hold values from -0.09375 to 0.09375
- weight_second: bfloat16 [3, 3, 512, 512], replicated, may hold values from -0.09375 to 0.09375
- weight_mix: bfloat16 [3, 3, 2048, 2048], P(None, None, None, 'rows'), may hold values from -0.046875 to 0.046875
- weight_out: bfloat16 [3, 3, 2048, 2048], P(None, None, 'rows'), may hold values from -0.046875 to 0.046875
Outputs:
- latent_out: bfloat16 [32, 4, 2048], P(('groups', 'rows')), parts along dimension 0
There are 2 independent parts, one for each index of `groups`. A program takes and returns all parts, laid end to end along the dimension named above; an argument that names none is the same for every part. Nothing has to cross between parts.
All inputs are finite; a program needn't handle non-finite values.
Results may differ from a plain program's by a relative error of at most 0.014.
Values may be sent and summed in bfloat16 or wider, within the bound.
A program may use at most 64 MiB of HBM per device.

v0:
```python
import jax
import jax.numpy as jnp
from jax import lax
from jax.sharding import PartitionSpec as P


def padded(value, sides, width):
    for axis, dim in sides:
        peers, length = (lax.axis_size(axis), value.shape[dim])
        up = [(i, (i + 1) % peers) for i in range(peers - 1)]
        down = [(j, i) for i, j in up]
        last = lax.slice_in_dim(value, length - width, length, axis=dim)
        first = lax.slice_in_dim(value, 0, width, axis=dim)
        before = lax.ppermute(last, axis, up)
        after = lax.ppermute(first, axis, down)
        value = jnp.concatenate([before, value, after], axis=dim)
    return value


def conv_rows(extended, weight):
    widened = jnp.pad(extended, ((0, 0), (1, 1), (0, 0)))
    row_count = extended.shape[0] - 2
    col_count = extended.shape[1]
    summed = jnp.zeros((row_count, col_count, weight.shape[3]), jnp.float32)
    for row_tap in range(3):
        for col_tap in range(3):
            summed = summed + jnp.dot(
                widened[row_tap : row_tap + row_count, col_tap : col_tap + col_count],
                weight[row_tap, col_tap],
                preferred_element_type=jnp.float32,
            )
    return summed


def conv_taps(feature, weight):
    row_count, col_count, in_count = feature.shape
    out_count = weight.shape[3]
    stacked = jnp.transpose(weight, (2, 0, 1, 3)).reshape(in_count, 9 * out_count)
    tap_terms = jnp.dot(
        feature.reshape(row_count * col_count, in_count),
        stacked,
        preferred_element_type=jnp.float32,
    )
    tap_terms = jnp.pad(
        tap_terms.reshape(row_count, col_count, 9 * out_count), ((1, 1), (1, 1), (0, 0))
    )
    summed = jnp.zeros((row_count, col_count, out_count), jnp.float32)
    for row_tap in range(3):
        for col_tap in range(3):
            lane_start = (3 * row_tap + col_tap) * out_count
            summed = (
                summed
                + tap_terms[
                    row_tap : row_tap + row_count,
                    col_tap : col_tap + col_count,
                    lane_start : lane_start + out_count,
                ]
            )
    return summed


def unshuffle_average(feature):
    row_count, col_count, chan_count = feature.shape
    widened = feature.astype(jnp.float32).reshape(row_count // 2, 2, col_count // 2, 2, chan_count)
    paired = (widened[:, :, :, 0] + widened[:, :, :, 1]) * 0.5
    return (
        jnp.transpose(paired, (0, 2, 3, 1))
        .reshape(row_count // 2, col_count // 2, 2 * chan_count)
        .astype(jnp.bfloat16)
    )


def halo_rows(feature):
    return padded(feature, (("rows", 0),), 1)


def pad_rows(feature):
    return jnp.pad(feature, ((1, 1), (0, 0), (0, 0)))


def local(pixels, weight_first, weight_second, weight_mix, weight_out):
    activated = jax.nn.silu(conv_rows(halo_rows(pixels), weight_first)).astype(jnp.bfloat16)
    block_out = (
        pixels.astype(jnp.float32) + conv_rows(halo_rows(activated), weight_second)
    ).astype(jnp.bfloat16)
    half_res = unshuffle_average(block_out)
    latent = unshuffle_average(half_res)
    whole_latent = lax.all_gather(latent, "rows", axis=0, tiled=True)
    hidden = jax.nn.silu(conv_taps(whole_latent, weight_mix)).astype(jnp.bfloat16)
    padded_hidden = pad_rows(hidden)
    mixed_sum = lax.psum_scatter(
        conv_rows(padded_hidden, weight_out), "rows", scatter_dimension=0, tiled=True
    )
    return (latent.astype(jnp.float32) + mixed_sum).astype(jnp.bfloat16)


def solution(mesh):
    return jax.shard_map(
        local,
        mesh=mesh,
        in_specs=(
            P(("groups", "rows"), None, None),
            P(),
            P(),
            P(None, None, None, "rows"),
            P(None, None, "rows", None),
        ),
        out_specs=P(("groups", "rows"), None, None),
        check_vma=False,
    )
```

profile of v0, /device:TPU:0, one launch (start us, length us, event | category | flops | bytes accessed | tf_op | source)
XLA Modules:
  0.0 194.3 jit_solution(849420155514540025)
XLA Ops:
  6.5 0.8 fusion.128
  7.3 2.3 %collective-permute-start = (bf16[1,16,512]{2,1,0:T(8,128)(2,1)S(1)}, bf16[1,16,512]{2,1,0:T(8,128)(2,1)S(1)}, u32[]{:S(2)}, u32[]{:S(2)}) collective-permute-start(bf16[1,16,512]{2,1,0:T(8,128)(2,1)S(1)} %get-tuple-element.9), channel_id=1, source_target_pairs={{0,1},{1,2},{2,3},{3,4},{4,5},{5,6},{6,7},{7,8},{8,9},{9,10},{10,1... | collective-permute-start | bytes 49160 | tf_op jit(solution)/shard_map/ppermute | solution.py:14
  9.7 1.3 collective-permute-start.1
  11.0 3.9 %collective-permute-done.1 = bf16[1,16,512]{2,1,0:T(8,128)(2,1)S(1)} collective-permute-done((bf16[1,16,512]{2,1,0:T(8,128)(2,1)S(1)}, bf16[1,16,512]{2,1,0:T(8,128)(2,1)S(1)}, u32[]{:S(2)}, u32[]{:S(2)}) %collective-permute-start.1) | collective-permute-done | bytes 16416 | tf_op jit(solution)/shard_map/ppermute | solution.py:15
  14.9 0.9 fusion.72
  15.8 1.2 fusion.27
  17.0 1.3 fusion.35
  18.3 1.2 convolution_add_fusion.21
  19.6 1.3 convolution_add_fusion.20
  20.9 1.2 convolution_add_fusion.19
  22.1 1.3 convolution_add_fusion.18
  23.4 1.3 convolution_add_fusion.17
  24.7 1.2 convolution_add_fusion.16
  25.9 1.3 multiply_convert_fusion.1
  27.2 4.4 %collective-permute-start.2 = (bf16[1,16,512]{2,1,0:T(8,128)(2,1)S(1)}, bf16[1,16,512]{2,1,0:T(8,128)(2,1)S(1)}, u32[]{:S(2)}, u32[]{:S(2)}) collective-permute-start(bf16[1,16,512]{2,1,0:T(8,128)(2,1)S(1)} %get-tuple-element.7), channel_id=1, source_target_pairs={{0,1},{1,2},{2,3},{3,4},{4,5},{5,6},{6,7},{7,8},{8,9},{9,10},{10,1... | collective-permute-start | bytes 49160 | tf_op jit(solution)/shard_map/ppermute | solution.py:14
  31.6 1.3 collective-permute-start.3
  32.9 6.8 %copy.38 = bf16[3,3,2048,128]{2,3,1,0:T(8,128)(2,1)} copy(bf16[3,3,2048,128]{3,2,1,0:T(8,128)(2,1)} %param.8) | data formatting | bytes 9437184 | tf_op args[3]
  39.7 1.2 fusion.16
  41.0 1.2 fusion.24
  42.2 1.2 convolution_add_fusion.15
  43.5 1.3 convolution_add_fusion.14
  44.8 1.2 convolution_add_fusion.13
  46.0 1.2 convolution_add_fusion.12
  47.3 1.3 convolution_add_fusion.11
  48.5 1.2 convolution_add_fusion.10
  49.8 1.3 fusion.5
  51.1 0.1 fusion.126
  51.2 2.7 %copy.45 = f32[2,2,8,1,512]{1,4,2,0,3:T(8,128)} copy(f32[2,2,8,1,512]{4,3,2,1,0:T(1,128)S(1)} %get-tuple-element.6) | data formatting | bytes 131072
  54.0 2.7 %copy.46 = f32[2,2,8,1,512]{1,4,2,0,3:T(8,128)} copy(f32[2,2,8,1,512]{4,3,2,1,0:T(1,128)S(1)} %get-tuple-element.5) | data formatting | bytes 131072
  56.6 6.0 %convert_bitcast_fusion = f32[2,8,512,2]{3,2,1,0:T(8,128)} fusion(f32[2,2,8,1,512]{1,4,2,0,3:T(8,128)} %copy.45, f32[2,2,8,1,512]{1,4,2,0,3:T(8,128)} %copy.46), kind=kLoop, calls=%fused_computation | loop fusion | flops 65536 | bytes 196608 | tf_op jit(solution)/shard_map/convert_element_type | solution.py:64
  62.6 4.1 %reshape.92 = f32[1,2,4,2,1024]{4,3,2,1,0:T(2,128)S(1)} reshape(f32[2,8,512,2]{3,2,1,0:T(8,128)} %convert_bitcast_fusion) | data formatting | bytes 131072 | tf_op jit(solution)/shard_map/convert_element_type | solution.py:64
  66.8 0.5 copy.35
  67.3 0.2 copy.36
  67.5 23.1 %all_gather.3 = bf16[16,4,2048]{2,1,0:T(4,128)(2,1)S(1)} all-gather(bf16[1,4,2048]{2,1,0:T(4,128)(2,1)S(1)} %copy.36), channel_id=1, replica_groups=mesh['groups'=2,'rows'=16] {'rows'}, dimensions={0}, use_global_device_ids=true | all-gather | bytes 278528 | tf_op jit(solution)/shard_map/all_gather | solution.py:88
  90.6 4.0 %fusion.66 = f32[16,4,1152]{2,0,1:T(8,128)S(1)} fusion(bf16[2048,1152,1]{0,1,2:T(8,128)(2,1)} %bitcast.162, bf16[16,4,2048]{2,1,0:T(4,128)(2,1)S(1)} %all_gather.3), kind=kOutput, calls=%fused_computation.100 | convolution fusion | flops 301989888 | bytes 5275648 | tf_op jit(solution)/shard_map/dot_general | solution.py:39
  94.8 0.2 fusion.14
  95.0 0.2 convolution_add_fusion.7
  95.2 0.2 convolution_add_fusion.6
  95.5 0.2 convolution_add_fusion.5
  95.7 0.2 convolution_add_fusion.4
  95.9 0.2 convolution_add_fusion.3
  96.1 0.2 convolution_add_fusion.2
  96.4 0.2 convolution_add_fusion.1
  96.6 0.2 convolution_add_fusion
  96.8 1.1 copy.41
  98.0 0.6 dynamic-slice
  98.6 86.9 %all-reduce.8.cloned.1.call-done = f32[16,4,2048]{2,1,0:T(4,128)} async-done(((f32[16,4,2048]{2,1,0:T(4,128)}), f32[16,4,2048]{2,1,0:T(4,128)}) %all-reduce.8.cloned.1.call-update) | async-done | bytes 524304
  185.5 1.9 fusion.108
  (21 shorter events, 0.3 us)
Async XLA Ops:
  6.5 19.4 %copy-start = (bf16[4,16,512]{2,1,0:T(8,128)(2,1)S(1)}, bf16[4,16,512]{2,1,0:T(8,128)(2,1)}, u32[]{:S(2)}) copy-start(bf16[4,16,512]{2,1,0:T(8,128)(2,1)} %param.5) | copy-start | bytes 196612
  6.5 179.0 %all-reduce.8.cloned.1.call-start = ((), (), s32[]{:S(2)}) async-start(), calls=%async_computation | async-start | bytes 1048576
  7.3 3.7 %collective-permute-start = (bf16[1,16,512]{2,1,0:T(8,128)(2,1)S(1)}, bf16[1,16,512]{2,1,0:T(8,128)(2,1)S(1)}, u32[]{:S(2)}, u32[]{:S(2)}) collective-permute-start(bf16[1,16,512]{2,1,0:T(8,128)(2,1)S(1)} %get-tuple-element.9), channel_id=1, source_target_pairs={{0,1},{1,2},{2,3},{3,4},{4,5},{5,6},{6,7},{7,8},{8,9},{9,10},{10,1... | collective-permute-start | bytes 49160 | tf_op jit(solution)/shard_map/ppermute | solution.py:14
  9.7 5.2 %collective-permute-start.1 = (bf16[1,16,512]{2,1,0:T(8,128)(2,1)S(1)}, bf16[1,16,512]{2,1,0:T(8,128)(2,1)S(1)}, u32[]{:S(2)}, u32[]{:S(2)}) collective-permute-start(bf16[1,16,512]{2,1,0:T(8,128)(2,1)S(1)} %get-tuple-element.10), channel_id=1, source_target_pairs={{1,0},{2,1},{3,2},{4,3},{5,4},{6,5},{7,6},{8,7},{9,8},{10,9},{11,1... | collective-permute-start | bytes 49160 | tf_op jit(solution)/shard_map/ppermute | solution.py:15
  27.2 12.4 %collective-permute-start.2 = (bf16[1,16,512]{2,1,0:T(8,128)(2,1)S(1)}, bf16[1,16,512]{2,1,0:T(8,128)(2,1)S(1)}, u32[]{:S(2)}, u32[]{:S(2)}) collective-permute-start(bf16[1,16,512]{2,1,0:T(8,128)(2,1)S(1)} %get-tuple-element.7), channel_id=1, source_target_pairs={{0,1},{1,2},{2,3},{3,4},{4,5},{5,6},{6,7},{7,8},{8,9},{9,10},{10,1... | collective-permute-start | bytes 49160 | tf_op jit(solution)/shard_map/ppermute | solution.py:14
  31.6 8.1 %collective-permute-start.3 = (bf16[1,16,512]{2,1,0:T(8,128)(2,1)S(1)}, bf16[1,16,512]{2,1,0:T(8,128)(2,1)S(1)}, u32[]{:S(2)}, u32[]{:S(2)}) collective-permute-start(bf16[1,16,512]{2,1,0:T(8,128)(2,1)S(1)} %get-tuple-element.8), channel_id=1, source_target_pairs={{1,0},{2,1},{3,2},{4,3},{5,4},{6,5},{7,6},{8,7},{9,8},{10,9},{11,1... | collective-permute-start | bytes 49160 | tf_op jit(solution)/shard_map/ppermute | solution.py:15
  90.6 4.1 %slice-start = ((s8[4718592]{0:T(1024)(128)(4,1)}), s8[4194304]{0:T(1024)(128)(4,1)S(1)}, s32[]{:S(2)}) async-start(s8[4718592]{0:T(1024)(128)(4,1)} %bitcast.163), calls=%async_computation.1 | async-start | bytes 8388608
  90.6 4.1 %slice-start.1 = ((s8[4718592]{0:T(1024)(128)(4,1)}), s8[524288]{0:T(1024)(128)(4,1)S(1)}, s32[]{:S(2)}) async-start(s8[4718592]{0:T(1024)(128)(4,1)} %bitcast.163), calls=%async_computation.2 | async-start | bytes 1048576
  95.7 2.3 %copy-start.1 = (u32[32]{0:T(128)S(1)}, u32[32]{0:T(128)}, u32[]{:S(2)}) copy-start(u32[32]{0:T(128)} %constant.26) | copy-start | bytes 388
Sparse Core Ops, SparseCore 0:
  98.1 87.3 all-reduce.7
where the time goes:
time: 196 us; the launch traced here: 194 us
  waiting for transfers between devices  90.8 us (46%)
  matrix products  28.6 us (15%)
  blocking collectives  23.1 us (12%)
  local copies, waits for them, and re-layouts  19.7 us (10%)
  between operations  13.8 us (7%)
  starting transfers between devices  9.31 us (5%)
  other arithmetic  8.97 us (5%)
    unnamed x2, waiting for transfers between devices  86.9 us
    dot_general x27, matrix products, conv_rows(): jnp.dot(widened[row_tap:row_tap + row_count, col_tap:col_tap + col_count]...  24.6 us
    all_gather x1, blocking collectives, local(): whole_latent = lax.all_gather(latent, 'rows', axis=0, tiled=True)  23.1 us
    unnamed x13, local copies, waits for them, and re-layouts  12.7 us
    ppermute x2, starting transfers between devices, padded(): before = lax.ppermute(last, axis, up)  6.72 us
    convert_element_type x1, other arithmetic, unshuffle_average(): feature.astype(jnp.float32)  6 us
    convert_element_type x1, local copies, waits for them, and re-layouts, unshuffle_average(): feature.astype(jnp.float32)  4.12 us
    dot_general x1, matrix products, conv_taps(): jnp.dot(feature.reshape(row_count * col_count, in_count), stacked, prefer...  4.03 us
  transfers between devices with their start and end apart: 5, of which 2 were waited for; matrix products, arithmetic and copies ran while one was open for 4% of the time, Pallas kernels for 0%

commit v1 on v0

v1 whole, which is shorter than its diff:
```python
import functools

import jax
import jax.numpy as jnp
from jax import lax
from jax.experimental import pallas as pl
from jax.experimental.pallas import tpu as pltpu
from jax.sharding import PartitionSpec as P

MESH = pl.DeviceIdType.MESH
BF16 = jnp.bfloat16
F32 = jnp.float32


def quotient(value, divisor):
    if divisor & (divisor - 1) == 0:
        return lax.shift_right_logical(value, divisor.bit_length() - 1)
    return value // divisor


def remainder(value, divisor):
    if divisor & (divisor - 1) == 0:
        return value & (divisor - 1)
    return value % divisor


def index(shape, dim):
    return lax.broadcasted_iota(jnp.int32, shape, dim)


def selection(mask, entry):
    return jnp.where(mask, entry, 0.0).astype(BF16)


def dot(left, right):
    return jnp.dot(left, right, preferred_element_type=F32)


def silu(value):
    return value / (1.0 + jnp.exp(-value))


def column_taps(value, cols):
    length = value.shape[0]
    col = remainder(index(value.shape, 0), cols)
    left = jnp.where(col == 0, 0.0, pltpu.roll(value, 1, 0))
    right = jnp.where(col == cols - 1, 0.0, pltpu.roll(value, length - 1, 0))
    return jnp.concatenate([left.astype(BF16), value.astype(BF16), right.astype(BF16)], axis=1)


def latent_tap(value, tap, rows, cols):
    row_step, col_step = tap // 3 - 1, tap % 3 - 1
    step = row_step * cols + col_step
    if step == 0:
        return value
    length = rows * cols
    place = index(value.shape, 0)
    row, col = quotient(place, cols) + row_step, remainder(place, cols) + col_step
    inside = (row >= 0) & (row < rows) & (col >= 0) & (col < cols)
    return jnp.where(inside, pltpu.roll(value, (-step) % length, 0), 0.0)


def kernel(
    n, px, w1, w2, wm, wo, out,
    ext, w1v, w2v, wmv, wov, mix_sel, sort_sel, back_sel, gathered, latents, outgoing, incoming,
    wsem, psem, hsend, hrecv, gsend, grecv, ssend, srecv,
):
    me = lax.axis_index("rows")
    rows, cols, ch = px.shape
    oc = wmv.shape[-1]
    lc = cols // 4
    nk = 16 // lc
    lw = 4 * ch // nk
    cw = ch // nk
    gs = min(n, 16)
    span = gs * lc
    pos = n * lc

    own_pixels = pltpu.make_async_copy(px, ext.at[pl.ds(2, rows)], psem)
    own_pixels.start()
    loads = []
    for which, (src, dst) in enumerate(((w1, w1v), (w2, w2v), (wm, wmv), (wo, wov))):
        loads.append([pltpu.make_async_copy(src.at[a], dst.at[a], wsem.at[which, a]) for a in range(3)])
        for load in loads[-1]:
            load.start()

    barrier = pltpu.get_barrier_semaphore()

    def greet(off, carry):
        pl.semaphore_signal(barrier, inc=1, device_id={"rows": lax.rem(me + off, n)}, device_id_type=MESH)
        return carry

    lax.fori_loop(1, n, greet, 0)

    blank = jnp.zeros((2, cols, ch), BF16)

    @pl.when(me == 0)
    def _():
        ext[pl.ds(0, 2)] = blank

    @pl.when(me == n - 1)
    def _():
        ext[pl.ds(rows + 2, 2)] = blank

    pl.semaphore_wait(barrier, n - 1)

    down = pltpu.make_async_remote_copy(
        src_ref=px.at[pl.ds(rows - 2, 2)], dst_ref=ext.at[pl.ds(0, 2)],
        send_sem=hsend.at[0], recv_sem=hrecv.at[0],
        device_id={"rows": lax.rem(me + 1, n)}, device_id_type=MESH,
    )
    up = pltpu.make_async_remote_copy(
        src_ref=px.at[pl.ds(0, 2)], dst_ref=ext.at[pl.ds(rows + 2, 2)],
        send_sem=hsend.at[1], recv_sem=hrecv.at[1],
        device_id={"rows": lax.rem(me + n - 1, n)}, device_id_type=MESH,
    )

    @pl.when(me < n - 1)
    def _():
        down.start()

    @pl.when(me > 0)
    def _():
        up.start()

    shape = (lw, lw)
    row, col = index(shape, 0), index(shape, 1)
    mix_sel[...] = selection(col == remainder(row, cw) * 4 + quotient(row, cw), 1.0)
    shape = (gs * 16, gs * 16)
    row, col = index(shape, 0), index(shape, 1)
    wanted = remainder(quotient(row, lc), gs) * 16 + quotient(row, span) * lc + remainder(row, lc)
    sort_sel[...] = selection(col == wanted, 1.0)
    wanted = remainder(quotient(row, lc), nk) * span + quotient(row, 16) * lc + remainder(row, lc)
    back_sel[...] = selection(col == wanted, 1.0)
    shape = (rows * cols // 2, rows * cols)
    pair_sel = selection(index(shape, 0) == quotient(index(shape, 1), 2), 0.5)
    shape = (64, rows * cols // 2)
    row, col = index(shape, 0), index(shape, 1)
    part = quotient(row, 16)
    strip = 2 * remainder(part, 2) + quotient(part, 2)
    quad_sel = selection(quotient(col, 2) == strip * lc + remainder(row, lc), 0.5)

    own_pixels.wait()

    @pl.when(me > 0)
    def _():
        down.wait_recv()

    @pl.when(me < n - 1)
    def _():
        up.wait_recv()

    pixels = ext[...].reshape((rows + 4) * cols, ch).astype(F32)
    taps = column_taps(pixels, cols)
    summed = jnp.zeros(((rows + 2) * cols, ch), F32)
    for a in range(3):
        loads[0][a].wait()
        summed = summed + dot(taps[a * cols : (a + rows + 2) * cols], w1v[a])
    row = quotient(index(summed.shape, 0), cols)
    outside = ((row == 0) & (me == 0)) | ((row == rows + 1) & (me == n - 1))
    activated = jnp.where(outside, 0.0, silu(summed)).astype(BF16)
    taps = column_taps(activated.astype(F32), cols)
    summed = pixels[2 * cols : (rows + 2) * cols]
    conv = jnp.zeros((rows * cols, ch), F32)
    for a in range(3):
        loads[1][a].wait()
        conv = conv + dot(taps[a * cols : (a + rows) * cols], w2v[a])
    block_out = (summed + conv).astype(BF16)

    half_res = dot(pair_sel, block_out).astype(BF16)
    quads = dot(quad_sel, half_res)
    chunk = quotient(index((16, cw), 0), lc)
    pieces = []
    for q in range(4):
        mine = quads[16 * q : 16 * q + 16]
        piece = mine[:, :cw]
        for k in range(1, nk):
            piece = jnp.where(chunk == k, mine[:, k * cw : (k + 1) * cw], piece)
        pieces.append(piece)
    latent = dot(jnp.concatenate(pieces, axis=1).astype(BF16), mix_sel[...]).astype(BF16)
    gathered[pl.ds(me, 1)] = latent[None]

    def exchange(source, target, send_sem, recv_sem, pick):
        def push(off, carry):
            peer = lax.rem(me + off, n)
            pltpu.make_async_remote_copy(
                src_ref=source.at[peer if pick else me], dst_ref=target.at[me],
                send_sem=send_sem.at[off], recv_sem=recv_sem.at[off],
                device_id={"rows": peer}, device_id_type=MESH,
            ).start()
            return carry

        def take(off, carry):
            peer = lax.rem(me + n - off, n)
            pltpu.make_async_remote_copy(
                src_ref=source.at[peer if pick else me], dst_ref=target.at[peer],
                send_sem=send_sem.at[off], recv_sem=recv_sem.at[off],
                device_id={"rows": peer}, device_id_type=MESH,
            ).wait_recv()
            return carry

        def settle(off, carry):
            peer = lax.rem(me + off, n)
            pltpu.make_async_remote_copy(
                src_ref=source.at[peer if pick else me], dst_ref=target.at[me],
                send_sem=send_sem.at[off], recv_sem=recv_sem.at[off],
                device_id={"rows": peer}, device_id_type=MESH,
            ).wait_send()
            return carry

        lax.fori_loop(1, n, push, 0)
        lax.fori_loop(1, n, take, 0)
        return lambda: lax.fori_loop(1, n, settle, 0)

    settle_latents = exchange(gathered, gathered, gsend, grecv, False)

    for g in range(n // gs):
        block = gathered[pl.ds(g * gs, gs)].reshape(gs * 16, lw)
        ordered = dot(sort_sel[...], block).astype(BF16)
        for k in range(nk):
            latents[pl.ds(g * span, span), pl.ds(k * lw, lw)] = ordered[k * span : (k + 1) * span]

    for load in loads[2]:
        load.wait()
    everywhere = latents[...]
    width = 2 if oc % 128 == 0 else 1
    hidden = jnp.zeros((pos, oc), F32)
    for first in range(0, 9, width):
        group = range(first, min(first + width, 9))
        weights = [wmv[tap // 3, tap % 3] for tap in group]
        weight = weights[0] if len(weights) == 1 else jnp.concatenate(weights, axis=1)
        terms = dot(everywhere, weight)
        for at, tap in enumerate(group):
            hidden = hidden + latent_tap(terms[:, at * oc : (at + 1) * oc], tap, n, lc)
    hidden = silu(hidden).astype(BF16).astype(F32)

    for load in loads[3]:
        load.wait()
    shifted = [latent_tap(hidden, tap, n, lc).astype(BF16) for tap in range(9)]
    parts = []
    if oc % 128 == 0:
        shifted = jnp.concatenate(shifted, axis=1)
        for k in range(nk):
            weight = wov[:, :, pl.ds(k * lw, lw)].reshape(9 * oc, lw)
            parts.append(dot(shifted, weight).astype(BF16))
    else:
        for k in range(nk):
            total = jnp.zeros((pos, lw), F32)
            for tap in range(9):
                total = total + dot(
                    shifted[tap], wov[tap // 3, pl.ds(tap % 3 * oc, oc), pl.ds(k * lw, lw)]
                )
            parts.append(total.astype(BF16))
    for g in range(n // gs):
        block = jnp.concatenate([part[g * span : (g + 1) * span] for part in parts], axis=0)
        outgoing[pl.ds(g * gs, gs)] = dot(back_sel[...], block).astype(BF16).reshape(gs, 16, lw)
    incoming[pl.ds(me, 1)] = outgoing[pl.ds(me, 1)]
    settle_sums = exchange(outgoing, incoming, ssend, srecv, True)
    total = latent.astype(F32) + jnp.sum(incoming[...].astype(F32), axis=0)
    for k in range(nk):
        out[0, :, pl.ds(k * lw, lw)] = total[k * lc : (k + 1) * lc].astype(BF16)

    @pl.when(me < n - 1)
    def _():
        down.wait_send()

    @pl.when(me > 0)
    def _():
        up.wait_send()

    settle_latents()
    settle_sums()


def local(n, pixels, weight_first, weight_second, weight_mix, weight_out):
    rows, cols, ch = pixels.shape
    cl, oc = weight_mix.shape[2:]
    lc = cols // 4
    nk = 16 // lc
    lw = cl // nk
    gs = min(n, 16)
    first = weight_first.reshape(3, 3 * ch, ch)
    second = weight_second.reshape(3, 3 * ch, ch)
    last = weight_out.reshape(3, 3 * oc, cl)
    dma = pltpu.SemaphoreType.DMA
    return pl.pallas_call(
        functools.partial(kernel, n),
        out_shape=jax.ShapeDtypeStruct((rows // 4, lc, cl), BF16),
        in_specs=[pl.BlockSpec(memory_space=pl.ANY)] * 5,
        out_specs=pl.BlockSpec(memory_space=pltpu.VMEM),
        scratch_shapes=[
            pltpu.VMEM((rows + 4, cols, ch), BF16),
            pltpu.VMEM(first.shape, BF16),
            pltpu.VMEM(second.shape, BF16),
            pltpu.VMEM(weight_mix.shape, BF16),
            pltpu.VMEM(last.shape, BF16),
            pltpu.VMEM((lw, lw), BF16),
            pltpu.VMEM((gs * 16, gs * 16), BF16),
            pltpu.VMEM((gs * 16, gs * 16), BF16),
            pltpu.VMEM((n, 16, lw), BF16),
            pltpu.VMEM((n * lc, cl), BF16),
            pltpu.VMEM((n, 16, lw), BF16),
            pltpu.VMEM((n, 16, lw), BF16),
            dma((4, 3)),
            dma,
            dma((2,)),
            dma((2,)),
            dma((n,)),
            dma((n,)),
            dma((n,)),
            dma((n,)),
        ],
        compiler_params=pltpu.CompilerParams(
            collective_id=0, has_side_effects=True, vmem_limit_bytes=56 * 1024 * 1024
        ),
    )(pixels, first, second, weight_mix, last)


def solution(mesh):
    return jax.shard_map(
        functools.partial(local, mesh.shape["rows"]),
        mesh=mesh,
        in_specs=(
            P(("groups", "rows"), None, None),
            P(),
            P(),
            P(None, None, None, "rows"),
            P(None, None, "rows", None),
        ),
        out_specs=P(("groups", "rows"), None, None),
        check_vma=False,
    )
```

time: 196 us -> 29.5 us (0.15)
  waiting for transfers between devices: 90.8 us -> 0 us
  matrix products: 28.6 us -> 0 us
  Pallas kernels: 0 us -> 27.6 us
  blocking collectives: 23.1 us -> 0 us
  local copies, waits for them, and re-layouts: 19.7 us -> 1.33 us
  between operations: 13.8 us -> 0.01 us
  starting transfers between devices: 9.31 us -> 0 us
  other arithmetic: 8.97 us -> 0 us
    unnamed x2 -> x0, waiting for transfers between devices: 86.9 us -> none
    dot_general x28 -> x0, matrix products: 28.6 us -> none  [the longest x27 24.6 us: conv_rows(): jnp.dot(widened[row_tap:row_tap + row_count, col_tap:col_tap + col_count]...]
    pallas_call x0 -> x1, Pallas kernels: none -> 27.6 us  [local(): pl.pallas_call(functools.partial(kernel, n), out_shape=jax.ShapeDtypeStru...]
    all_gather x1 -> x0, blocking collectives: 23.1 us -> none  [local(): whole_latent = lax.all_gather(latent, 'rows', axis=0, tiled=True)]
    unnamed x13 -> x1, local copies, waits for them, and re-layouts: 12.7 us -> 1.33 us
    ppermute x4 -> x0, starting transfers between devices: 9.31 us -> none  [the longest x2 6.72 us: padded(): before = lax.ppermute(last, axis, up)]
    convert_element_type x4 -> x0, other arithmetic: 8.03 us -> none  [the longest x1 6 us: unshuffle_average(): feature.astype(jnp.float32)]
    convert_element_type x3 -> x0, local copies, waits for them, and re-layouts: 4.82 us -> none  [the longest x1 4.12 us: unshuffle_average(): feature.astype(jnp.float32)]
  transfers between devices with their start and end apart: 5 -> 0, of which waited for: 2 -> 0; matrix products, arithmetic and copies ran while one was open for 4% -> 0% of each run, Pallas kernels for 0% -> 0%
where the time goes in v1:
time: 29.5 us; the launch traced here: 28.9 us
  Pallas kernels  27.6 us (94%)
  local copies, waits for them, and re-layouts  1.33 us (5%)
    pallas_call x1, Pallas kernels, local(): pl.pallas_call(functools.partial(kernel, n), out_shape=jax.ShapeDtypeStru...  27.6 us
    unnamed x1, local copies, waits for them, and re-layouts  1.33 us

profile of v1, /device:TPU:0, one launch (start us, length us, event | category | flops | bytes accessed | tf_op | source)
XLA Modules:
  0.0 28.9 jit_solution(16520400436411057699)
XLA Ops:
  0.0 27.6 %shard_map.55 = bf16[1,4,2048]{2,1,0:T(4,128)(2,1)} custom-call(bf16[4,16,512]{2,1,0:T(8,128)(2,1)} %px.1, bf16[3,1536,512]{2,1,0:T(8,128)(2,1)} %bitcast.3, bf16[3,1536,512]{2,1,0:T(8,128)(2,1)} %bitcast.4, bf16[3,3,2048,128]{3,2,1,0:T(8,128)(2,1)} %wm.1, bf16[3,384,2048]{2,1,0:T(8,128)(2,1)} %bitcast.5), custom_call_target="tpu_custom_call" | custom-call | tf_op jit(solution)/shard_map/pallas_call | solution.py:286
  27.6 1.3 %copy.7 = bf16[1,4,2048]{2,1,0:T(4,128)(2,1)} copy(bf16[1,4,2048]{2,1,0:T(4,128)(2,1)} %shard_map.55) | data formatting | bytes 32768

commit v2 on v1

--- a/solution.py
+++ b/solution.py
@@ -62,10 +62,12 @@
 
 def kernel(
     n, px, w1, w2, wm, wo, out,
-    ext, w1v, w2v, wmv, wov, mix_sel, sort_sel, back_sel, gathered, latents, outgoing, incoming,
-    wsem, psem, hsend, hrecv, gsend, grecv, ssend, srecv,
+    ext, w1v, w2v, wmv, wov, mix_sel, sort_sel, back_sel, gathered, latents, outgoing, swapped, paired, incoming,
+    wsem, psem, hsend, hrecv, gsend, grecv, fsend, frecv, xsend, xrecv, ssend, srecv,
 ):
     me = lax.axis_index("rows")
+    core, chip, chips = lax.rem(me, 2), lax.div(me, 2), n // 2
+    sibling = me + 1 - 2 * core
     rows, cols, ch = px.shape
     oc = wmv.shape[-1]
     lc = cols // 4
@@ -75,6 +77,10 @@
     gs = min(n, 16)
     span = gs * lc
     pos = n * lc
+    hw = lw // 2
+
+    def twin(off):
+        return 2 * lax.rem(chip + off, chips) + core
 
     own_pixels = pltpu.make_async_copy(px, ext.at[pl.ds(2, rows)], psem)
     own_pixels.start()
@@ -86,11 +92,16 @@
 
     barrier = pltpu.get_barrier_semaphore()
 
-    def greet(off, carry):
-        pl.semaphore_signal(barrier, inc=1, device_id={"rows": lax.rem(me + off, n)}, device_id_type=MESH)
+    def greet(peer):
+        pl.semaphore_signal(barrier, inc=1, device_id={"rows": peer}, device_id_type=MESH)
+
+    def greet_chip(off, carry):
+        greet(twin(off))
         return carry
 
-    lax.fori_loop(1, n, greet, 0)
+    greet(lax.rem(jnp.where(core == 0, me + n - 1, me + 1), n))
+    greet(sibling)
+    lax.fori_loop(1, chips, greet_chip, 0)
 
     blank = jnp.zeros((2, cols, ch), BF16)
 
@@ -102,7 +113,7 @@
     def _():
         ext[pl.ds(rows + 2, 2)] = blank
 
-    pl.semaphore_wait(barrier, n - 1)
+    pl.semaphore_wait(barrier, chips + 1)
 
     down = pltpu.make_async_remote_copy(
         src_ref=px.at[pl.ds(rows - 2, 2)], dst_ref=ext.at[pl.ds(0, 2)],
@@ -130,7 +141,9 @@
     row, col = index(shape, 0), index(shape, 1)
     wanted = remainder(quotient(row, lc), gs) * 16 + quotient(row, span) * lc + remainder(row, lc)
     sort_sel[...] = selection(col == wanted, 1.0)
-    wanted = remainder(quotient(row, lc), nk) * span + quotient(row, 16) * lc + remainder(row, lc)
+    place = quotient(row, 16)
+    place = 2 * remainder(place, gs // 2) + quotient(place, gs // 2)
+    wanted = remainder(quotient(row, lc), nk) * span + place * lc + remainder(row, lc)
     back_sel[...] = selection(col == wanted, 1.0)
     shape = (rows * cols // 2, rows * cols)
     pair_sel = selection(index(shape, 0) == quotient(index(shape, 1), 2), 0.5)
@@ -180,39 +193,46 @@
     latent = dot(jnp.concatenate(pieces, axis=1).astype(BF16), mix_sel[...]).astype(BF16)
     gathered[pl.ds(me, 1)] = latent[None]
 
-    def exchange(source, target, send_sem, recv_sem, pick):
-        def push(off, carry):
-            peer = lax.rem(me + off, n)
-            pltpu.make_async_remote_copy(
-                src_ref=source.at[peer if pick else me], dst_ref=target.at[me],
-                send_sem=send_sem.at[off], recv_sem=recv_sem.at[off],
-                device_id={"rows": peer}, device_id_type=MESH,
-            ).start()
-            return carry
-
-        def take(off, carry):
-            peer = lax.rem(me + n - off, n)
-            pltpu.make_async_remote_copy(
-                src_ref=source.at[peer if pick else me], dst_ref=target.at[peer],
-                send_sem=send_sem.at[off], recv_sem=recv_sem.at[off],
-                device_id={"rows": peer}, device_id_type=MESH,
-            ).wait_recv()
-            return carry
-
-        def settle(off, carry):
-            peer = lax.rem(me + off, n)
-            pltpu.make_async_remote_copy(
-                src_ref=source.at[peer if pick else me], dst_ref=target.at[me],
-                send_sem=send_sem.at[off], recv_sem=recv_sem.at[off],
-                device_id={"rows": peer}, device_id_type=MESH,
-            ).wait_send()
-            return carry
-
-        lax.fori_loop(1, n, push, 0)
-        lax.fori_loop(1, n, take, 0)
-        return lambda: lax.fori_loop(1, n, settle, 0)
-
-    settle_latents = exchange(gathered, gathered, gsend, grecv, False)
+    def handover(off):
+        slot = gathered.at[twin(off)]
+        return pltpu.make_async_remote_copy(
+            src_ref=slot, dst_ref=slot, send_sem=fsend.at[off], recv_sem=frecv.at[off],
+            device_id={"rows": sibling}, device_id_type=MESH,
+        )
+
+    def spread(off, slot):
+        return pltpu.make_async_remote_copy(
+            src_ref=gathered.at[slot], dst_ref=gathered.at[slot],
+            send_sem=gsend.at[off], recv_sem=grecv.at[off],
+            device_id={"rows": twin(off)}, device_id_type=MESH,
+        )
+
+    def push_latent(off, carry):
+        spread(off, me).start()
+        return carry
+
+    def pass_on(off, carry):
+        spread(off, twin(chips - off)).wait_recv()
+        handover(chips - off).start()
+        return carry
+
+    def take_latent(off, carry):
+        slot = gathered.at[2 * lax.rem(chip + off, chips) + 1 - core]
+        pltpu.make_async_remote_copy(
+            src_ref=slot, dst_ref=slot, send_sem=fsend.at[off], recv_sem=frecv.at[off],
+            device_id={"rows": sibling}, device_id_type=MESH,
+        ).wait_recv()
+        return carry
+
+    def settle_latent(off, carry):
+        spread(off, me).wait_send()
+        handover(off).wait_send()
+        return carry
+
+    lax.fori_loop(1, chips, push_latent, 0)
+    handover(0).start()
+    lax.fori_loop(1, chips, pass_on, 0)
+    lax.fori_loop(0, chips, take_latent, 0)
 
     for g in range(n // gs):
         block = gathered[pl.ds(g * gs, gs)].reshape(gs * 16, lw)
@@ -237,28 +257,69 @@
     for load in loads[3]:
         load.wait()
     shifted = [latent_tap(hidden, tap, n, lc).astype(BF16) for tap in range(9)]
-    parts = []
     if oc % 128 == 0:
         shifted = jnp.concatenate(shifted, axis=1)
+
+    def contribution(start):
+        lanes = pl.ds(start, hw)
+        if oc % 128 == 0:
+            return dot(shifted, wov[:, :, lanes].reshape(9 * oc, hw)).astype(BF16)
+        total = jnp.zeros((pos, hw), F32)
+        for tap in range(9):
+            total = total + dot(shifted[tap], wov[tap // 3, pl.ds(tap % 3 * oc, oc), lanes])
+        return total.astype(BF16)
+
+    def swap(h):
+        return pltpu.make_async_remote_copy(
+            src_ref=outgoing.at[h, 1 - core], dst_ref=swapped.at[h],
+            send_sem=xsend.at[h], recv_sem=xrecv.at[h],
+            device_id={"rows": sibling}, device_id_type=MESH,
+        )
+
+    def scatter(h, off, slot):
+        return pltpu.make_async_remote_copy(
+            src_ref=paired.at[h, lax.rem(chip + off, chips)], dst_ref=incoming.at[h, slot],
+            send_sem=ssend.at[h, off], recv_sem=srecv.at[h, off],
+            device_id={"rows": twin(off)}, device_id_type=MESH,
+        )
+
+    def multiply(h):
+        parts = [contribution((h * nk + k) * hw) for k in range(nk)]
+        for g in range(n // gs):
+            block = jnp.concatenate([part[g * span : (g + 1) * span] for part in parts], axis=0)
+            block = dot(back_sel[...], block).astype(BF16).reshape(2, gs // 2, 16, hw)
+            outgoing[h, :, pl.ds(g * gs // 2, gs // 2)] = block
+        swap(h).start()
+
+    def send_sums(h):
+        swap(h).wait_recv()
+        paired[h] = (outgoing[h, core].astype(F32) + swapped[h].astype(F32)).astype(BF16)
+
+        def push_sum(off, carry):
+            scatter(h, off, chip).start()
+            return carry
+
+        lax.fori_loop(1, chips, push_sum, 0)
+        incoming[h, pl.ds(chip, 1)] = paired[h, pl.ds(chip, 1)]
+
+    multiply(0)
+    multiply(1)
+    send_sums(0)
+    send_sums(1)
+
+    residual = latent.astype(F32)
+    for h in range(2):
+
+        def take_sum(off, carry):
+            scatter(h, off, lax.rem(chip + chips - off, chips)).wait_recv()
+            return carry
+
+        lax.fori_loop(1, chips, take_sum, 0)
+        total = jnp.sum(incoming[h].astype(F32), axis=0)
         for k in range(nk):
-            weight = wov[:, :, pl.ds(k * lw, lw)].reshape(9 * oc, lw)
-            parts.append(dot(shifted, weight).astype(BF16))
-    else:
-        for k in range(nk):
-            total = jnp.zeros((pos, lw), F32)
-            for tap in range(9):
-                total = total + dot(
-                    shifted[tap], wov[tap // 3, pl.ds(tap % 3 * oc, oc), pl.ds(k * lw, lw)]
-                )
-            parts.append(total.astype(BF16))
-    for g in range(n // gs):
-        block = jnp.concatenate([part[g * span : (g + 1) * span] for part in parts], axis=0)
-        outgoing[pl.ds(g * gs, gs)] = dot(back_sel[...], block).astype(BF16).reshape(gs, 16, lw)
-    incoming[pl.ds(me, 1)] = outgoing[pl.ds(me, 1)]
-    settle_sums = exchange(outgoing, incoming, ssend, srecv, True)
-    total = latent.astype(F32) + jnp.sum(incoming[...].astype(F32), axis=0)
-    for k in range(nk):
-        out[0, :, pl.ds(k * lw, lw)] = total[k * lc : (k + 1) * lc].astype(BF16)
+            whole = h * nk + k
+            piece = residual[whole // 2 * lc : (whole // 2 + 1) * lc, whole % 2 * hw : (whole % 2 + 1) * hw]
+            out[0, :, pl.ds(whole * hw, hw)] = (total[k * lc : (k + 1) * lc] + piece).astype(BF16)
 
     @pl.when(me < n - 1)
     def _():
@@ -268,8 +329,16 @@
     def _():
         up.wait_send()
 
-    settle_latents()
-    settle_sums()
+    handover(0).wait_send()
+    lax.fori_loop(1, chips, settle_latent, 0)
+    for h in range(2):
+        swap(h).wait_send()
+
+        def settle_sum(off, carry):
+            scatter(h, off, chip).wait_send()
+            return carry
+
+        lax.fori_loop(1, chips, settle_sum, 0)
 
 
 def local(n, pixels, weight_first, weight_second, weight_mix, weight_out):
@@ -299,16 +368,22 @@
             pltpu.VMEM((gs * 16, gs * 16), BF16),
             pltpu.VMEM((n, 16, lw), BF16),
             pltpu.VMEM((n * lc, cl), BF16),
-            pltpu.VMEM((n, 16, lw), BF16),
-            pltpu.VMEM((n, 16, lw), BF16),
+            pltpu.VMEM((2, 2, n // 2, 16, lw // 2), BF16),
+            pltpu.VMEM((2, n // 2, 16, lw // 2), BF16),
+            pltpu.VMEM((2, n // 2, 16, lw // 2), BF16),
+            pltpu.VMEM((2, n // 2, 16, lw // 2), BF16),
             dma((4, 3)),
             dma,
             dma((2,)),
             dma((2,)),
-            dma((n,)),
-            dma((n,)),
-            dma((n,)),
-            dma((n,)),
+            dma((n // 2,)),
+            dma((n // 2,)),
+            dma((n // 2,)),
+            dma((n // 2,)),
+            dma((2,)),
+            dma((2,)),
+            dma((2, n // 2)),
+            dma((2, n // 2)),
         ],
         compiler_params=pltpu.CompilerParams(
             collective_id=0, has_side_effects=True, vmem_limit_bytes=56 * 1024 * 1024

time: 29.5 us -> 28.4 us (0.963); the launches traced: 28.9 us -> 28.2 us
  Pallas kernels: 27.6 us -> 26.8 us
    pallas_call x1, Pallas kernels: 27.6 us -> 26.8 us  [local(): pl.pallas_call(functools.partial(kernel, n), out_shape=jax.ShapeDtypeStru...]
where the time goes in v2:
time: 28.4 us; the launch traced here: 28.2 us
  Pallas kernels  26.8 us (94%)
  local copies, waits for them, and re-layouts  1.33 us (5%)
    pallas_call x1, Pallas kernels, local(): pl.pallas_call(functools.partial(kernel, n), out_shape=jax.ShapeDtypeStru...  26.8 us
    unnamed x1, local copies, waits for them, and re-layouts  1.33 us

profile of v2, /device:TPU:0, one launch (start us, length us, event | category | flops | bytes accessed | tf_op | source)
XLA Modules:
  0.0 28.2 jit_solution(15063486132178499784)
XLA Ops:
  0.0 26.8 %shard_map.55 = bf16[1,4,2048]{2,1,0:T(4,128)(2,1)} custom-call(bf16[4,16,512]{2,1,0:T(8,128)(2,1)} %px.1, bf16[3,1536,512]{2,1,0:T(8,128)(2,1)} %bitcast.3, bf16[3,1536,512]{2,1,0:T(8,128)(2,1)} %bitcast.4, bf16[3,3,2048,128]{3,2,1,0:T(8,128)(2,1)} %wm.1, bf16[3,384,2048]{2,1,0:T(8,128)(2,1)} %bitcast.5), custom_call_target="tpu_custom_call" | custom-call | tf_op jit(solution)/shard_map/pallas_call | solution.py:355
  26.8 1.3 %copy.7 = bf16[1,4,2048]{2,1,0:T(4,128)(2,1)} copy(bf16[1,4,2048]{2,1,0:T(4,128)(2,1)} %shard_map.55) | data formatting | bytes 32768

commit v3 on v2

--- a/solution.py
+++ b/solution.py
@@ -87,8 +87,8 @@
     loads = []
     for which, (src, dst) in enumerate(((w1, w1v), (w2, w2v), (wm, wmv), (wo, wov))):
         loads.append([pltpu.make_async_copy(src.at[a], dst.at[a], wsem.at[which, a]) for a in range(3)])
-        for load in loads[-1]:
-            load.start()
+    for load in loads[0] + loads[1]:
+        load.start()
 
     barrier = pltpu.get_barrier_semaphore()
 
@@ -163,6 +163,9 @@
     def _():
         up.wait_recv()
 
+    for load in loads[2] + loads[3]:
+        load.start()
+
     pixels = ext[...].reshape((rows + 4) * cols, ch).astype(F32)
     taps = column_taps(pixels, cols)
     summed = jnp.zeros(((rows + 2) * cols, ch), F32)
@@ -307,6 +310,16 @@
     send_sums(0)
     send_sums(1)
 
+    @pl.when(me < n - 1)
+    def _():
+        down.wait_send()
+
+    @pl.when(me > 0)
+    def _():
+        up.wait_send()
+
+    handover(0).wait_send()
+    lax.fori_loop(1, chips, settle_latent, 0)
     residual = latent.astype(F32)
     for h in range(2):
 
@@ -321,16 +334,6 @@
             piece = residual[whole // 2 * lc : (whole // 2 + 1) * lc, whole % 2 * hw : (whole % 2 + 1) * hw]
             out[0, :, pl.ds(whole * hw, hw)] = (total[k * lc : (k + 1) * lc] + piece).astype(BF16)
 
-    @pl.when(me < n - 1)
-    def _():
-        down.wait_send()
-
-    @pl.when(me > 0)
-    def _():
-        up.wait_send()
-
-    handover(0).wait_send()
-    lax.fori_loop(1, chips, settle_latent, 0)
     for h in range(2):
         swap(h).wait_send()
 

time: 28.4 us -> 28.2 us (level)
  no operation moved by 1% of the time
where the time goes in v3:
time: 28.2 us; the launch traced here: 27.9 us
  Pallas kernels  26.6 us (94%)
  local copies, waits for them, and re-layouts  1.33 us (5%)
    pallas_call x1, Pallas kernels, local(): pl.pallas_call(functools.partial(kernel, n), out_shape=jax.ShapeDtypeStru...  26.6 us
    unnamed x1, local copies, waits for them, and re-layouts  1.33 us

profile of v3, /device:TPU:0, one launch (start us, length us, event | category | flops | bytes accessed | tf_op | source)
XLA Modules:
  0.0 27.9 jit_solution(4267371381545784935)
XLA Ops:
  0.0 26.6 %shard_map.55 = bf16[1,4,2048]{2,1,0:T(4,128)(2,1)} custom-call(bf16[4,16,512]{2,1,0:T(8,128)(2,1)} %px.1, bf16[3,1536,512]{2,1,0:T(8,128)(2,1)} %bitcast.3, bf16[3,1536,512]{2,1,0:T(8,128)(2,1)} %bitcast.4, bf16[3,3,2048,128]{3,2,1,0:T(8,128)(2,1)} %wm.1, bf16[3,384,2048]{2,1,0:T(8,128)(2,1)} %bitcast.5), custom_call_target="tpu_custom_call" | custom-call | tf_op jit(solution)/shard_map/pallas_call | solution.py:358
  26.6 1.3 %copy.7 = bf16[1,4,2048]{2,1,0:T(4,128)(2,1)} copy(bf16[1,4,2048]{2,1,0:T(4,128)(2,1)} %shard_map.55) | data formatting | bytes 32768

commit v4 on v3

--- a/solution.py
+++ b/solution.py
@@ -73,7 +73,7 @@
     lc = cols // 4
     nk = 16 // lc
     lw = 4 * ch // nk
-    cw = ch // nk
+    cw = ch // (2 * nk)
     gs = min(n, 16)
     span = gs * lc
     pos = n * lc
@@ -134,9 +134,9 @@
     def _():
         up.start()
 
-    shape = (lw, lw)
+    shape = (2 * ch, hw)
     row, col = index(shape, 0), index(shape, 1)
-    mix_sel[...] = selection(col == remainder(row, cw) * 4 + quotient(row, cw), 1.0)
+    mix_sel[...] = selection(col == remainder(row, cw) * 4 + quotient(row, ch // 2), 1.0)
     shape = (gs * 16, gs * 16)
     row, col = index(shape, 0), index(shape, 1)
     wanted = remainder(quotient(row, lc), gs) * 16 + quotient(row, span) * lc + remainder(row, lc)
@@ -176,85 +176,93 @@
     outside = ((row == 0) & (me == 0)) | ((row == rows + 1) & (me == n - 1))
     activated = jnp.where(outside, 0.0, silu(summed)).astype(BF16)
     taps = column_taps(activated.astype(F32), cols)
-    summed = pixels[2 * cols : (rows + 2) * cols]
-    conv = jnp.zeros((rows * cols, ch), F32)
-    for a in range(3):
-        loads[1][a].wait()
-        conv = conv + dot(taps[a * cols : (a + rows) * cols], w2v[a])
-    block_out = (summed + conv).astype(BF16)
-
-    half_res = dot(pair_sel, block_out).astype(BF16)
-    quads = dot(quad_sel, half_res)
-    chunk = quotient(index((16, cw), 0), lc)
-    pieces = []
-    for q in range(4):
-        mine = quads[16 * q : 16 * q + 16]
-        piece = mine[:, :cw]
-        for k in range(1, nk):
-            piece = jnp.where(chunk == k, mine[:, k * cw : (k + 1) * cw], piece)
-        pieces.append(piece)
-    latent = dot(jnp.concatenate(pieces, axis=1).astype(BF16), mix_sel[...]).astype(BF16)
-    gathered[pl.ds(me, 1)] = latent[None]
-
-    def handover(off):
-        slot = gathered.at[twin(off)]
+    own = pixels[2 * cols : (rows + 2) * cols]
+    for load in loads[1]:
+        load.wait()
+    chunk = quotient(index((16, ch // 2), 0), lc) == quotient(index((16, ch // 2), 1), cw)
+
+    def make_latent(h):
+        lanes = slice(h * ch // 2, (h + 1) * ch // 2)
+        conv = dot(taps[: rows * cols], w2v[0, :, lanes])
+        for a in range(1, 3):
+            conv = conv + dot(taps[a * cols : (a + rows) * cols], w2v[a, :, lanes])
+        block_out = (own[:, lanes] + conv).astype(BF16)
+        half_res = dot(pair_sel, block_out).astype(BF16)
+        quads = dot(quad_sel, half_res)
+        pieces = [jnp.where(chunk, quads[16 * q : 16 * q + 16], 0.0).astype(BF16) for q in range(4)]
+        return dot(jnp.concatenate(pieces, axis=1), mix_sel[...]).astype(BF16)
+
+    def handover(h, off):
+        slot = gathered.at[h, twin(off)]
         return pltpu.make_async_remote_copy(
-            src_ref=slot, dst_ref=slot, send_sem=fsend.at[off], recv_sem=frecv.at[off],
+            src_ref=slot, dst_ref=slot, send_sem=fsend.at[h, off], recv_sem=frecv.at[h, off],
             device_id={"rows": sibling}, device_id_type=MESH,
         )
 
-    def spread(off, slot):
+    def spread(h, off, slot):
         return pltpu.make_async_remote_copy(
-            src_ref=gathered.at[slot], dst_ref=gathered.at[slot],
-            send_sem=gsend.at[off], recv_sem=grecv.at[off],
+            src_ref=gathered.at[h, slot], dst_ref=gathered.at[h, slot],
+            send_sem=gsend.at[h, off], recv_sem=grecv.at[h, off],
             device_id={"rows": twin(off)}, device_id_type=MESH,
         )
 
-    def push_latent(off, carry):
-        spread(off, me).start()
-        return carry
-
-    def pass_on(off, carry):
-        spread(off, twin(chips - off)).wait_recv()
-        handover(chips - off).start()
-        return carry
-
-    def take_latent(off, carry):
-        slot = gathered.at[2 * lax.rem(chip + off, chips) + 1 - core]
-        pltpu.make_async_remote_copy(
-            src_ref=slot, dst_ref=slot, send_sem=fsend.at[off], recv_sem=frecv.at[off],
-            device_id={"rows": sibling}, device_id_type=MESH,
-        ).wait_recv()
-        return carry
-
-    def settle_latent(off, carry):
-        spread(off, me).wait_send()
-        handover(off).wait_send()
-        return carry
-
-    lax.fori_loop(1, chips, push_latent, 0)
-    handover(0).start()
-    lax.fori_loop(1, chips, pass_on, 0)
-    lax.fori_loop(0, chips, take_latent, 0)
-
-    for g in range(n // gs):
-        block = gathered[pl.ds(g * gs, gs)].reshape(gs * 16, lw)
-        ordered = dot(sort_sel[...], block).astype(BF16)
-        for k in range(nk):
-            latents[pl.ds(g * span, span), pl.ds(k * lw, lw)] = ordered[k * span : (k + 1) * span]
+    def send_latent(h):
+        def push_latent(off, carry):
+            spread(h, off, me).start()
+            return carry
+
+        lax.fori_loop(1, chips, push_latent, 0)
+        handover(h, 0).start()
+
+    def forward_latents(h):
+        def pass_on(off, carry):
+            spread(h, off, twin(chips - off)).wait_recv()
+            handover(h, chips - off).start()
+            return carry
+
+        lax.fori_loop(1, chips, pass_on, 0)
+
+    def take_latents(h):
+        def take_latent(off, carry):
+            slot = gathered.at[h, 2 * lax.rem(chip + off, chips) + 1 - core]
+            pltpu.make_async_remote_copy(
+                src_ref=slot, dst_ref=slot, send_sem=fsend.at[h, off], recv_sem=frecv.at[h, off],
+                device_id={"rows": sibling}, device_id_type=MESH,
+            ).wait_recv()
+            return carry
+
+        lax.fori_loop(0, chips, take_latent, 0)
+        for g in range(n // gs):
+            block = gathered[h, pl.ds(g * gs, gs)].reshape(gs * 16, hw)
+            ordered = dot(sort_sel[...], block).astype(BF16)
+            for k in range(nk):
+                latents[h, pl.ds(g * span, span), pl.ds(k * hw, hw)] = ordered[k * span : (k + 1) * span]
+
+    own_latents = []
+    for h in range(2):
+        own_latents.append(make_latent(h))
+        gathered[h, pl.ds(me, 1)] = own_latents[h][None]
+        send_latent(h)
+    forward_latents(0)
+    forward_latents(1)
 
     for load in loads[2]:
         load.wait()
-    everywhere = latents[...]
     width = 2 if oc % 128 == 0 else 1
+    groups = [range(first, min(first + width, 9)) for first in range(0, 9, width)]
+    terms = [None] * len(groups)
+    for h in range(2):
+        take_latents(h)
+        everywhere = latents[h]
+        for at, group in enumerate(groups):
+            weights = [wmv[tap // 3, tap % 3, pl.ds(h * nk * hw, nk * hw)] for tap in group]
+            weight = weights[0] if len(weights) == 1 else jnp.concatenate(weights, axis=1)
+            term = dot(everywhere, weight)
+            terms[at] = term if h == 0 else terms[at] + term
     hidden = jnp.zeros((pos, oc), F32)
-    for first in range(0, 9, width):
-        group = range(first, min(first + width, 9))
-        weights = [wmv[tap // 3, tap % 3] for tap in group]
-        weight = weights[0] if len(weights) == 1 else jnp.concatenate(weights, axis=1)
-        terms = dot(everywhere, weight)
+    for term, group in zip(terms, groups):
         for at, tap in enumerate(group):
-            hidden = hidden + latent_tap(terms[:, at * oc : (at + 1) * oc], tap, n, lc)
+            hidden = hidden + latent_tap(term[:, at * oc : (at + 1) * oc], tap, n, lc)
     hidden = silu(hidden).astype(BF16).astype(F32)
 
     for load in loads[3]:
@@ -318,9 +326,15 @@
     def _():
         up.wait_send()
 
-    handover(0).wait_send()
-    lax.fori_loop(1, chips, settle_latent, 0)
-    residual = latent.astype(F32)
+    for h in range(2):
+
+        def settle_latent(off, carry):
+            spread(h, off, me).wait_send()
+            handover(h, off).wait_send()
+            return carry
+
+        handover(h, 0).wait_send()
+        lax.fori_loop(1, chips, settle_latent, 0)
     for h in range(2):
 
         def take_sum(off, carry):
@@ -328,11 +342,9 @@
             return carry
 
         lax.fori_loop(1, chips, take_sum, 0)
-        total = jnp.sum(incoming[h].astype(F32), axis=0)
+        total = jnp.sum(incoming[h].astype(F32), axis=0) + own_latents[h].astype(F32)
         for k in range(nk):
-            whole = h * nk + k
-            piece = residual[whole // 2 * lc : (whole // 2 + 1) * lc, whole % 2 * hw : (whole % 2 + 1) * hw]
-            out[0, :, pl.ds(whole * hw, hw)] = (total[k * lc : (k + 1) * lc] + piece).astype(BF16)
+            out[0, :, pl.ds((h * nk + k) * hw, hw)] = total[k * lc : (k + 1) * lc].astype(BF16)
 
     for h in range(2):
         swap(h).wait_send()
@@ -366,11 +378,11 @@
             pltpu.VMEM(second.shape, BF16),
             pltpu.VMEM(weight_mix.shape, BF16),
             pltpu.VMEM(last.shape, BF16),
-            pltpu.VMEM((lw, lw), BF16),
+            pltpu.VMEM((2 * ch, lw // 2), BF16),
             pltpu.VMEM((gs * 16, gs * 16), BF16),
             pltpu.VMEM((gs * 16, gs * 16), BF16),
-            pltpu.VMEM((n, 16, lw), BF16),
-            pltpu.VMEM((n * lc, cl), BF16),
+            pltpu.VMEM((2, n, 16, lw // 2), BF16),
+            pltpu.VMEM((2, n * lc, cl // 2), BF16),
             pltpu.VMEM((2, 2, n // 2, 16, lw // 2), BF16),
             pltpu.VMEM((2, n // 2, 16, lw // 2), BF16),
             pltpu.VMEM((2, n // 2, 16, lw // 2), BF16),
@@ -379,10 +391,10 @@
             dma,
             dma((2,)),
             dma((2,)),
-            dma((n // 2,)),
-            dma((n // 2,)),
-            dma((n // 2,)),
-            dma((n // 2,)),
+            dma((2, n // 2)),
+            dma((2, n // 2)),
+            dma((2, n // 2)),
+            dma((2, n // 2)),
             dma((2,)),
             dma((2,)),
             dma((2, n // 2)),

time: 28.2 us -> 28.3 us (level)
  no operation moved by 1% of the time
where the time goes in v4:
time: 28.3 us; the launch traced here: 28 us
  Pallas kernels  26.7 us (94%)
  local copies, waits for them, and re-layouts  1.33 us (5%)
    pallas_call x1, Pallas kernels, local(): pl.pallas_call(functools.partial(kernel, n), out_shape=jax.ShapeDtypeStru...  26.7 us
    unnamed x1, local copies, waits for them, and re-layouts  1.33 us

profile of v4, /device:TPU:0, one launch (start us, length us, event | category | flops | bytes accessed | tf_op | source)
XLA Modules:
  0.0 28.0 jit_solution(16318683031438010501)
XLA Ops:
  0.0 26.7 %shard_map.55 = bf16[1,4,2048]{2,1,0:T(4,128)(2,1)} custom-call(bf16[4,16,512]{2,1,0:T(8,128)(2,1)} %px.1, bf16[3,1536,512]{2,1,0:T(8,128)(2,1)} %bitcast.3, bf16[3,1536,512]{2,1,0:T(8,128)(2,1)} %bitcast.4, bf16[3,3,2048,128]{3,2,1,0:T(8,128)(2,1)} %wm.1, bf16[3,384,2048]{2,1,0:T(8,128)(2,1)} %bitcast.5), custom_call_target="tpu_custom_call" | custom-call | tf_op jit(solution)/shard_map/pallas_call | solution.py:370
  26.7 1.3 %copy.7 = bf16[1,4,2048]{2,1,0:T(4,128)(2,1)} copy(bf16[1,4,2048]{2,1,0:T(4,128)(2,1)} %shard_map.55) | data formatting | bytes 32768

commit v5 on v3

--- a/solution.py
+++ b/solution.py
@@ -88,7 +88,7 @@
     for which, (src, dst) in enumerate(((w1, w1v), (w2, w2v), (wm, wmv), (wo, wov))):
         loads.append([pltpu.make_async_copy(src.at[a], dst.at[a], wsem.at[which, a]) for a in range(3)])
     for load in loads[0] + loads[1]:
-        load.start()
+        load.start(priority=1)
 
     barrier = pltpu.get_barrier_semaphore()
 
@@ -164,7 +164,7 @@
         up.wait_recv()
 
     for load in loads[2] + loads[3]:
-        load.start()
+        load.start(priority=1)
 
     pixels = ext[...].reshape((rows + 4) * cols, ch).astype(F32)
     taps = column_taps(pixels, cols)

time: 28.2 us -> 28.2 us (level)
  no operation moved by 1% of the time
where the time goes in v5:
time: 28.2 us; the launch traced here: 27.9 us
  Pallas kernels  26.6 us (94%)
  local copies, waits for them, and re-layouts  1.33 us (5%)
    pallas_call x1, Pallas kernels, local(): pl.pallas_call(functools.partial(kernel, n), out_shape=jax.ShapeDtypeStru...  26.6 us
    unnamed x1, local copies, waits for them, and re-layouts  1.33 us

profile of v5, /device:TPU:0, one launch (start us, length us, event | category | flops | bytes accessed | tf_op | source)
XLA Modules:
  0.0 27.9 jit_solution(7964439921121312740)
XLA Ops:
  0.0 26.6 %shard_map.55 = bf16[1,4,2048]{2,1,0:T(4,128)(2,1)} custom-call(bf16[4,16,512]{2,1,0:T(8,128)(2,1)} %px.1, bf16[3,1536,512]{2,1,0:T(8,128)(2,1)} %bitcast.3, bf16[3,1536,512]{2,1,0:T(8,128)(2,1)} %bitcast.4, bf16[3,3,2048,128]{3,2,1,0:T(8,128)(2,1)} %wm.1, bf16[3,384,2048]{2,1,0:T(8,128)(2,1)} %bitcast.5), custom_call_target="tpu_custom_call" | custom-call | tf_op jit(solution)/shard_map/pallas_call | solution.py:358
  26.6 1.3 %copy.7 = bf16[1,4,2048]{2,1,0:T(4,128)(2,1)} copy(bf16[1,4,2048]{2,1,0:T(4,128)(2,1)} %shard_map.55) | data formatting | bytes 32768

commit v6 on v3

--- a/solution.py
+++ b/solution.py
@@ -60,14 +60,28 @@
     return jnp.where(inside, pltpu.roll(value, (-step) % length, 0), 0.0)
 
 
+def each(count, body):
+    if count <= 16:
+        for off in range(1, count):
+            body(off)
+        return
+
+    def step(off, carry):
+        body(off)
+        return carry
+
+    lax.fori_loop(1, count, step, 0)
+
+
 def kernel(
     n, px, w1, w2, wm, wo, out,
     ext, w1v, w2v, wmv, wov, mix_sel, sort_sel, back_sel, gathered, latents, outgoing, swapped, paired, incoming,
     wsem, psem, hsend, hrecv, gsend, grecv, fsend, frecv, xsend, xrecv, ssend, srecv,
 ):
     me = lax.axis_index("rows")
-    core, chip, chips = lax.rem(me, 2), lax.div(me, 2), n // 2
+    core, chip, chips = me & 1, lax.shift_right_logical(me, 1), n // 2
     sibling = me + 1 - 2 * core
+    even = chips & (chips - 1) == 0
     rows, cols, ch = px.shape
     oc = wmv.shape[-1]
     lc = cols // 4
@@ -79,8 +93,11 @@
     pos = n * lc
     hw = lw // 2
 
+    def chip_at(off):
+        return chip ^ off if even else lax.rem(chip + off, chips)
+
     def twin(off):
-        return 2 * lax.rem(chip + off, chips) + core
+        return 2 * chip_at(off) + core
 
     own_pixels = pltpu.make_async_copy(px, ext.at[pl.ds(2, rows)], psem)
     own_pixels.start()
@@ -95,13 +112,10 @@
     def greet(peer):
         pl.semaphore_signal(barrier, inc=1, device_id={"rows": peer}, device_id_type=MESH)
 
-    def greet_chip(off, carry):
-        greet(twin(off))
-        return carry
-
-    greet(lax.rem(jnp.where(core == 0, me + n - 1, me + 1), n))
+    before, after = jnp.where(me == 0, n - 1, me - 1), jnp.where(me == n - 1, 0, me + 1)
+    greet(jnp.where(core == 0, before, after))
     greet(sibling)
-    lax.fori_loop(1, chips, greet_chip, 0)
+    each(chips, lambda off: greet(twin(off)))
 
     blank = jnp.zeros((2, cols, ch), BF16)
 
@@ -118,12 +132,12 @@
     down = pltpu.make_async_remote_copy(
         src_ref=px.at[pl.ds(rows - 2, 2)], dst_ref=ext.at[pl.ds(0, 2)],
         send_sem=hsend.at[0], recv_sem=hrecv.at[0],
-        device_id={"rows": lax.rem(me + 1, n)}, device_id_type=MESH,
+        device_id={"rows": after}, device_id_type=MESH,
     )
     up = pltpu.make_async_remote_copy(
         src_ref=px.at[pl.ds(0, 2)], dst_ref=ext.at[pl.ds(rows + 2, 2)],
         send_sem=hsend.at[1], recv_sem=hrecv.at[1],
-        device_id={"rows": lax.rem(me + n - 1, n)}, device_id_type=MESH,
+        device_id={"rows": before}, device_id_type=MESH,
     )
 
     @pl.when(me < n - 1)
@@ -139,7 +153,9 @@
     mix_sel[...] = selection(col == remainder(row, cw) * 4 + quotient(row, cw), 1.0)
     shape = (gs * 16, gs * 16)
     row, col = index(shape, 0), index(shape, 1)
-    wanted = remainder(quotient(row, lc), gs) * 16 + quotient(row, span) * lc + remainder(row, lc)
+    place = remainder(quotient(row, lc), gs)
+    place = remainder(place, 2) * (gs // 2) + quotient(place, 2)
+    wanted = place * 16 + quotient(row, span) * lc + remainder(row, lc)
     sort_sel[...] = selection(col == wanted, 1.0)
     place = quotient(row, 16)
     place = 2 * remainder(place, gs // 2) + quotient(place, gs // 2)
@@ -194,51 +210,33 @@
             piece = jnp.where(chunk == k, mine[:, k * cw : (k + 1) * cw], piece)
         pieces.append(piece)
     latent = dot(jnp.concatenate(pieces, axis=1).astype(BF16), mix_sel[...]).astype(BF16)
-    gathered[pl.ds(me, 1)] = latent[None]
-
-    def handover(off):
-        slot = gathered.at[twin(off)]
-        return pltpu.make_async_remote_copy(
-            src_ref=slot, dst_ref=slot, send_sem=fsend.at[off], recv_sem=frecv.at[off],
-            device_id={"rows": sibling}, device_id_type=MESH,
-        )
-
-    def spread(off, slot):
-        return pltpu.make_async_remote_copy(
-            src_ref=gathered.at[slot], dst_ref=gathered.at[slot],
-            send_sem=gsend.at[off], recv_sem=grecv.at[off],
+    gathered[core, pl.ds(chip, 1)] = latent[None]
+
+    handover = pltpu.make_async_remote_copy(
+        src_ref=gathered.at[core], dst_ref=gathered.at[core], send_sem=fsend, recv_sem=frecv,
+        device_id={"rows": sibling}, device_id_type=MESH,
+    )
+    others = gathered.at[core, pl.ds(0, chips - 1)]
+    spread = pltpu.make_async_remote_copy(
+        src_ref=others, dst_ref=others, send_sem=gsend, recv_sem=grecv,
+        device_id={"rows": sibling}, device_id_type=MESH,
+    )
+
+    def push_latent(off):
+        slot = gathered.at[core, chip]
+        pltpu.make_async_remote_copy(
+            src_ref=slot, dst_ref=slot, send_sem=gsend, recv_sem=grecv,
             device_id={"rows": twin(off)}, device_id_type=MESH,
-        )
-
-    def push_latent(off, carry):
-        spread(off, me).start()
-        return carry
-
-    def pass_on(off, carry):
-        spread(off, twin(chips - off)).wait_recv()
-        handover(chips - off).start()
-        return carry
-
-    def take_latent(off, carry):
-        slot = gathered.at[2 * lax.rem(chip + off, chips) + 1 - core]
-        pltpu.make_async_remote_copy(
-            src_ref=slot, dst_ref=slot, send_sem=fsend.at[off], recv_sem=frecv.at[off],
-            device_id={"rows": sibling}, device_id_type=MESH,
-        ).wait_recv()
-        return carry
-
-    def settle_latent(off, carry):
-        spread(off, me).wait_send()
-        handover(off).wait_send()
-        return carry
-
-    lax.fori_loop(1, chips, push_latent, 0)
-    handover(0).start()
-    lax.fori_loop(1, chips, pass_on, 0)
-    lax.fori_loop(0, chips, take_latent, 0)
+        ).start()
+
+    each(chips, push_latent)
+    if chips > 1:
+        spread.wait_recv()
+    handover.start()
+    handover.wait_recv()
 
     for g in range(n // gs):
-        block = gathered[pl.ds(g * gs, gs)].reshape(gs * 16, lw)
+        block = gathered[:, pl.ds(g * gs // 2, gs // 2)].reshape(gs * 16, lw)
         ordered = dot(sort_sel[...], block).astype(BF16)
         for k in range(nk):
             latents[pl.ds(g * span, span), pl.ds(k * lw, lw)] = ordered[k * span : (k + 1) * span]
@@ -279,11 +277,12 @@
             device_id={"rows": sibling}, device_id_type=MESH,
         )
 
-    def scatter(h, off, slot):
+    def scatter(h):
+        several = pl.ds(0, chips - 1)
         return pltpu.make_async_remote_copy(
-            src_ref=paired.at[h, lax.rem(chip + off, chips)], dst_ref=incoming.at[h, slot],
-            send_sem=ssend.at[h, off], recv_sem=srecv.at[h, off],
-            device_id={"rows": twin(off)}, device_id_type=MESH,
+            src_ref=paired.at[h, several], dst_ref=incoming.at[h, several],
+            send_sem=ssend.at[h], recv_sem=srecv.at[h],
+            device_id={"rows": sibling}, device_id_type=MESH,
         )
 
     def multiply(h):
@@ -298,12 +297,15 @@
         swap(h).wait_recv()
         paired[h] = (outgoing[h, core].astype(F32) + swapped[h].astype(F32)).astype(BF16)
 
-        def push_sum(off, carry):
-            scatter(h, off, chip).start()
-            return carry
-
-        lax.fori_loop(1, chips, push_sum, 0)
-        incoming[h, pl.ds(chip, 1)] = paired[h, pl.ds(chip, 1)]
+        def push_sum(off):
+            pltpu.make_async_remote_copy(
+                src_ref=paired.at[h, chip_at(off)], dst_ref=incoming.at[h, off],
+                send_sem=ssend.at[h], recv_sem=srecv.at[h],
+                device_id={"rows": twin(off)}, device_id_type=MESH,
+            ).start()
+
+        each(chips, push_sum)
+        incoming[h, pl.ds(0, 1)] = paired[h, pl.ds(chip, 1)]
 
     multiply(0)
     multiply(1)
@@ -318,16 +320,13 @@
     def _():
         up.wait_send()
 
-    handover(0).wait_send()
-    lax.fori_loop(1, chips, settle_latent, 0)
+    handover.wait_send()
+    if chips > 1:
+        spread.wait_send()
     residual = latent.astype(F32)
     for h in range(2):
-
-        def take_sum(off, carry):
-            scatter(h, off, lax.rem(chip + chips - off, chips)).wait_recv()
-            return carry
-
-        lax.fori_loop(1, chips, take_sum, 0)
+        if chips > 1:
+            scatter(h).wait_recv()
         total = jnp.sum(incoming[h].astype(F32), axis=0)
         for k in range(nk):
             whole = h * nk + k
@@ -336,12 +335,8 @@
 
     for h in range(2):
         swap(h).wait_send()
-
-        def settle_sum(off, carry):
-            scatter(h, off, chip).wait_send()
-            return carry
-
-        lax.fori_loop(1, chips, settle_sum, 0)
+        if chips > 1:
+            scatter(h).wait_send()
 
 
 def local(n, pixels, weight_first, weight_second, weight_mix, weight_out):
@@ -369,7 +364,7 @@
             pltpu.VMEM((lw, lw), BF16),
             pltpu.VMEM((gs * 16, gs * 16), BF16),
             pltpu.VMEM((gs * 16, gs * 16), BF16),
-            pltpu.VMEM((n, 16, lw), BF16),
+            pltpu.VMEM((2, n // 2, 16, lw), BF16),
             pltpu.VMEM((n * lc, cl), BF16),
             pltpu.VMEM((2, 2, n // 2, 16, lw // 2), BF16),
             pltpu.VMEM((2, n // 2, 16, lw // 2), BF16),
@@ -379,14 +374,14 @@
             dma,
             dma((2,)),
             dma((2,)),
-            dma((n // 2,)),
-            dma((n // 2,)),
-            dma((n // 2,)),
-            dma((n // 2,)),
-            dma((2,)),
-            dma((2,)),
-            dma((2, n // 2)),
-            dma((2, n // 2)),
+            dma,
+            dma,
+            dma,
+            dma,
+            dma((2,)),
+            dma((2,)),
+            dma((2,)),
+            dma((2,)),
         ],
         compiler_params=pltpu.CompilerParams(
             collective_id=0, has_side_effects=True, vmem_limit_bytes=56 * 1024 * 1024

time: 28.2 us -> 28 us (level)
  no operation moved by 1% of the time
where the time goes in v6:
time: 28 us; the launch traced here: 27.8 us
  Pallas kernels  26.4 us (94%)
  local copies, waits for them, and re-layouts  1.33 us (5%)
    pallas_call x1, Pallas kernels, local(): pl.pallas_call(functools.partial(kernel, n), out_shape=jax.ShapeDtypeStru...  26.4 us
    unnamed x1, local copies, waits for them, and re-layouts  1.33 us

profile of v6, /device:TPU:0, one launch (start us, length us, event | category | flops | bytes accessed | tf_op | source)
XLA Modules:
  0.0 27.8 jit_solution(786904094892025183)
XLA Ops:
  0.0 26.4 %shard_map.55 = bf16[1,4,2048]{2,1,0:T(4,128)(2,1)} custom-call(bf16[4,16,512]{2,1,0:T(8,128)(2,1)} %px.1, bf16[3,1536,512]{2,1,0:T(8,128)(2,1)} %bitcast.3, bf16[3,1536,512]{2,1,0:T(8,128)(2,1)} %bitcast.4, bf16[3,3,2048,128]{3,2,1,0:T(8,128)(2,1)} %wm.1, bf16[3,384,2048]{2,1,0:T(8,128)(2,1)} %bitcast.5), custom_call_target="tpu_custom_call" | custom-call | tf_op jit(solution)/shard_map/pallas_call | solution.py:353
  26.4 1.3 %copy.7 = bf16[1,4,2048]{2,1,0:T(4,128)(2,1)} copy(bf16[1,4,2048]{2,1,0:T(4,128)(2,1)} %shard_map.55) | data formatting | bytes 32768

commit v7 on v6

--- a/solution.py
+++ b/solution.py
@@ -103,9 +103,23 @@
     own_pixels.start()
     loads = []
     for which, (src, dst) in enumerate(((w1, w1v), (w2, w2v), (wm, wmv), (wo, wov))):
-        loads.append([pltpu.make_async_copy(src.at[a], dst.at[a], wsem.at[which, a]) for a in range(3)])
-    for load in loads[0] + loads[1]:
-        load.start()
+        loads.append([])
+        depth = src.shape[-2]
+        pieces = 2 if depth % 32 == 0 else 1
+        for a in range(3):
+            for half in range(pieces):
+                part = pl.ds(half * depth // pieces, depth // pieces)
+                place = (a, slice(None), part) if len(src.shape) == 4 else (a, part)
+                loads[-1].append(
+                    pltpu.make_async_copy(src.at[place], dst.at[place], wsem.at[which, 2 * a + half])
+                )
+
+    def start_loads(which):
+        for at, load in enumerate(loads[which]):
+            load.start(priority=at % 2)
+
+    start_loads(0)
+    start_loads(1)
 
     barrier = pltpu.get_barrier_semaphore()
 
@@ -147,6 +161,9 @@
     @pl.when(me > 0)
     def _():
         up.start()
+
+    start_loads(2)
+    start_loads(3)
 
     shape = (lw, lw)
     row, col = index(shape, 0), index(shape, 1)
@@ -179,14 +196,12 @@
     def _():
         up.wait_recv()
 
-    for load in loads[2] + loads[3]:
-        load.start()
-
     pixels = ext[...].reshape((rows + 4) * cols, ch).astype(F32)
     taps = column_taps(pixels, cols)
     summed = jnp.zeros(((rows + 2) * cols, ch), F32)
     for a in range(3):
-        loads[0][a].wait()
+        for load in loads[0][a * len(loads[0]) // 3 : (a + 1) * len(loads[0]) // 3]:
+            load.wait()
         summed = summed + dot(taps[a * cols : (a + rows + 2) * cols], w1v[a])
     row = quotient(index(summed.shape, 0), cols)
     outside = ((row == 0) & (me == 0)) | ((row == rows + 1) & (me == n - 1))
@@ -195,7 +210,8 @@
     summed = pixels[2 * cols : (rows + 2) * cols]
     conv = jnp.zeros((rows * cols, ch), F32)
     for a in range(3):
-        loads[1][a].wait()
+        for load in loads[1][a * len(loads[1]) // 3 : (a + 1) * len(loads[1]) // 3]:
+            load.wait()
         conv = conv + dot(taps[a * cols : (a + rows) * cols], w2v[a])
     block_out = (summed + conv).astype(BF16)
 
@@ -370,7 +386,7 @@
             pltpu.VMEM((2, n // 2, 16, lw // 2), BF16),
             pltpu.VMEM((2, n // 2, 16, lw // 2), BF16),
             pltpu.VMEM((2, n // 2, 16, lw // 2), BF16),
-            dma((4, 3)),
+            dma((4, 6)),
             dma,
             dma((2,)),
             dma((2,)),

time: 28 us -> 28.2 us (level)
  no operation moved by 1% of the time
where the time goes in v7:
time: 28.2 us; the launch traced here: 27.9 us
  Pallas kernels  26.6 us (94%)
  local copies, waits for them, and re-layouts  1.33 us (5%)
    pallas_call x1, Pallas kernels, local(): pl.pallas_call(functools.partial(kernel, n), out_shape=jax.ShapeDtypeStru...  26.6 us
    unnamed x1, local copies, waits for them, and re-layouts  1.33 us

profile of v7, /device:TPU:0, one launch (start us, length us, event | category | flops | bytes accessed | tf_op | source)
XLA Modules:
  0.0 27.9 jit_solution(11480742150552815533)
XLA Ops:
  0.0 26.6 %shard_map.55 = bf16[1,4,2048]{2,1,0:T(4,128)(2,1)} custom-call(bf16[4,16,512]{2,1,0:T(8,128)(2,1)} %px.1, bf16[3,1536,512]{2,1,0:T(8,128)(2,1)} %bitcast.3, bf16[3,1536,512]{2,1,0:T(8,128)(2,1)} %bitcast.4, bf16[3,3,2048,128]{3,2,1,0:T(8,128)(2,1)} %wm.1, bf16[3,384,2048]{2,1,0:T(8,128)(2,1)} %bitcast.5), custom_call_target="tpu_custom_call" | custom-call | tf_op jit(solution)/shard_map/pallas_call | solution.py:369
  26.6 1.3 %copy.7 = bf16[1,4,2048]{2,1,0:T(4,128)(2,1)} copy(bf16[1,4,2048]{2,1,0:T(4,128)(2,1)} %shard_map.55) | data formatting | bytes 32768

commit v8 on v6

--- a/solution.py
+++ b/solution.py
@@ -87,7 +87,7 @@
     lc = cols // 4
     nk = 16 // lc
     lw = 4 * ch // nk
-    cw = ch // nk
+    cw = ch // (2 * nk)
     gs = min(n, 16)
     span = gs * lc
     pos = n * lc
@@ -148,9 +148,84 @@
     def _():
         up.start()
 
-    shape = (lw, lw)
+    shape = (2 * ch, hw)
     row, col = index(shape, 0), index(shape, 1)
-    mix_sel[...] = selection(col == remainder(row, cw) * 4 + quotient(row, cw), 1.0)
+    mix_sel[...] = selection(col == remainder(row, cw) * 4 + quotient(row, ch // 2), 1.0)
+    shape = (rows * cols // 2, rows * cols)
+    pair_sel = selection(index(shape, 0) == quotient(index(shape, 1), 2), 0.5)
+    shape = (64, rows * cols // 2)
+    row, col = index(shape, 0), index(shape, 1)
+    part = quotient(row, 16)
+    strip = 2 * remainder(part, 2) + quotient(part, 2)
+    quad_sel = selection(quotient(col, 2) == strip * lc + remainder(row, lc), 0.5)
+
+    own_pixels.wait()
+
+    @pl.when(me > 0)
+    def _():
+        down.wait_recv()
+
+    @pl.when(me < n - 1)
+    def _():
+        up.wait_recv()
+
+    for load in loads[2] + loads[3]:
+        load.start()
+
+    pixels = ext[...].reshape((rows + 4) * cols, ch).astype(F32)
+    taps = column_taps(pixels, cols)
+    summed = jnp.zeros(((rows + 2) * cols, ch), F32)
+    for a in range(3):
+        loads[0][a].wait()
+        summed = summed + dot(taps[a * cols : (a + rows + 2) * cols], w1v[a])
+    row = quotient(index(summed.shape, 0), cols)
+    outside = ((row == 0) & (me == 0)) | ((row == rows + 1) & (me == n - 1))
+    activated = jnp.where(outside, 0.0, silu(summed)).astype(BF16)
+    taps = column_taps(activated.astype(F32), cols)
+    own = pixels[2 * cols : (rows + 2) * cols]
+    for load in loads[1]:
+        load.wait()
+    chunk = quotient(index((16, ch // 2), 0), lc) == quotient(index((16, ch // 2), 1), cw)
+
+    def make_latent(h):
+        lanes = slice(h * ch // 2, (h + 1) * ch // 2)
+        conv = dot(taps[: rows * cols], w2v[0, :, lanes])
+        for a in range(1, 3):
+            conv = conv + dot(taps[a * cols : (a + rows) * cols], w2v[a, :, lanes])
+        block_out = (own[:, lanes] + conv).astype(BF16)
+        half_res = dot(pair_sel, block_out).astype(BF16)
+        quads = dot(quad_sel, half_res)
+        pieces = [jnp.where(chunk, quads[16 * q : 16 * q + 16], 0.0).astype(BF16) for q in range(4)]
+        return dot(jnp.concatenate(pieces, axis=1), mix_sel[...]).astype(BF16)
+
+    def handover(h):
+        return pltpu.make_async_remote_copy(
+            src_ref=gathered.at[h, core], dst_ref=gathered.at[h, core],
+            send_sem=fsend.at[h], recv_sem=frecv.at[h],
+            device_id={"rows": sibling}, device_id_type=MESH,
+        )
+
+    def spread(h):
+        others = gathered.at[h, core, pl.ds(0, chips - 1)]
+        return pltpu.make_async_remote_copy(
+            src_ref=others, dst_ref=others, send_sem=gsend.at[h], recv_sem=grecv.at[h],
+            device_id={"rows": sibling}, device_id_type=MESH,
+        )
+
+    own_latents = []
+    for h in range(2):
+        own_latents.append(make_latent(h))
+        gathered[h, core, pl.ds(chip, 1)] = own_latents[h][None]
+        slot = gathered.at[h, core, chip]
+
+        def push_latent(off):
+            pltpu.make_async_remote_copy(
+                src_ref=slot, dst_ref=slot, send_sem=gsend.at[h], recv_sem=grecv.at[h],
+                device_id={"rows": twin(off)}, device_id_type=MESH,
+            ).start()
+
+        each(chips, push_latent)
+
     shape = (gs * 16, gs * 16)
     row, col = index(shape, 0), index(shape, 1)
     place = remainder(quotient(row, lc), gs)
@@ -161,98 +236,33 @@
     place = 2 * remainder(place, gs // 2) + quotient(place, gs // 2)
     wanted = remainder(quotient(row, lc), nk) * span + place * lc + remainder(row, lc)
     back_sel[...] = selection(col == wanted, 1.0)
-    shape = (rows * cols // 2, rows * cols)
-    pair_sel = selection(index(shape, 0) == quotient(index(shape, 1), 2), 0.5)
-    shape = (64, rows * cols // 2)
-    row, col = index(shape, 0), index(shape, 1)
-    part = quotient(row, 16)
-    strip = 2 * remainder(part, 2) + quotient(part, 2)
-    quad_sel = selection(quotient(col, 2) == strip * lc + remainder(row, lc), 0.5)
-
-    own_pixels.wait()
-
-    @pl.when(me > 0)
-    def _():
-        down.wait_recv()
-
-    @pl.when(me < n - 1)
-    def _():
-        up.wait_recv()
-
-    for load in loads[2] + loads[3]:
-        load.start()
-
-    pixels = ext[...].reshape((rows + 4) * cols, ch).astype(F32)
-    taps = column_taps(pixels, cols)
-    summed = jnp.zeros(((rows + 2) * cols, ch), F32)
-    for a in range(3):
-        loads[0][a].wait()
-        summed = summed + dot(taps[a * cols : (a + rows + 2) * cols], w1v[a])
-    row = quotient(index(summed.shape, 0), cols)
-    outside = ((row == 0) & (me == 0)) | ((row == rows + 1) & (me == n - 1))
-    activated = jnp.where(outside, 0.0, silu(summed)).astype(BF16)
-    taps = column_taps(activated.astype(F32), cols)
-    summed = pixels[2 * cols : (rows + 2) * cols]
-    conv = jnp.zeros((rows * cols, ch), F32)
-    for a in range(3):
-        loads[1][a].wait()
-        conv = conv + dot(taps[a * cols : (a + rows) * cols], w2v[a])
-    block_out = (summed + conv).astype(BF16)
-
-    half_res = dot(pair_sel, block_out).astype(BF16)
-    quads = dot(quad_sel, half_res)
-    chunk = quotient(index((16, cw), 0), lc)
-    pieces = []
-    for q in range(4):
-        mine = quads[16 * q : 16 * q + 16]
-        piece = mine[:, :cw]
-        for k in range(1, nk):
-            piece = jnp.where(chunk == k, mine[:, k * cw : (k + 1) * cw], piece)
-        pieces.append(piece)
-    latent = dot(jnp.concatenate(pieces, axis=1).astype(BF16), mix_sel[...]).astype(BF16)
-    gathered[core, pl.ds(chip, 1)] = latent[None]
-
-    handover = pltpu.make_async_remote_copy(
-        src_ref=gathered.at[core], dst_ref=gathered.at[core], send_sem=fsend, recv_sem=frecv,
-        device_id={"rows": sibling}, device_id_type=MESH,
-    )
-    others = gathered.at[core, pl.ds(0, chips - 1)]
-    spread = pltpu.make_async_remote_copy(
-        src_ref=others, dst_ref=others, send_sem=gsend, recv_sem=grecv,
-        device_id={"rows": sibling}, device_id_type=MESH,
-    )
-
-    def push_latent(off):
-        slot = gathered.at[core, chip]
-        pltpu.make_async_remote_copy(
-            src_ref=slot, dst_ref=slot, send_sem=gsend, recv_sem=grecv,
-            device_id={"rows": twin(off)}, device_id_type=MESH,
-        ).start()
-
-    each(chips, push_latent)
-    if chips > 1:
-        spread.wait_recv()
-    handover.start()
-    handover.wait_recv()
-
-    for g in range(n // gs):
-        block = gathered[:, pl.ds(g * gs // 2, gs // 2)].reshape(gs * 16, lw)
-        ordered = dot(sort_sel[...], block).astype(BF16)
-        for k in range(nk):
-            latents[pl.ds(g * span, span), pl.ds(k * lw, lw)] = ordered[k * span : (k + 1) * span]
-
     for load in loads[2]:
         load.wait()
-    everywhere = latents[...]
+    for h in range(2):
+        if chips > 1:
+            spread(h).wait_recv()
+        handover(h).start()
+
     width = 2 if oc % 128 == 0 else 1
+    groups = [range(first, min(first + width, 9)) for first in range(0, 9, width)]
+    terms = [None] * len(groups)
+    for h in range(2):
+        handover(h).wait_recv()
+        for g in range(n // gs):
+            block = gathered[h, :, pl.ds(g * gs // 2, gs // 2)].reshape(gs * 16, hw)
+            ordered = dot(sort_sel[...], block).astype(BF16)
+            for k in range(nk):
+                latents[h, pl.ds(g * span, span), pl.ds(k * hw, hw)] = ordered[k * span : (k + 1) * span]
+        everywhere = latents[h]
+        for at, group in enumerate(groups):
+            weights = [wmv[tap // 3, tap % 3, pl.ds(h * nk * hw, nk * hw)] for tap in group]
+            weight = weights[0] if len(weights) == 1 else jnp.concatenate(weights, axis=1)
+            term = dot(everywhere, weight)
+            terms[at] = term if h == 0 else terms[at] + term
     hidden = jnp.zeros((pos, oc), F32)
-    for first in range(0, 9, width):
-        group = range(first, min(first + width, 9))
-        weights = [wmv[tap // 3, tap % 3] for tap in group]
-        weight = weights[0] if len(weights) == 1 else jnp.concatenate(weights, axis=1)
-        terms = dot(everywhere, weight)
+    for term, group in zip(terms, groups):
         for at, tap in enumerate(group):
-            hidden = hidden + latent_tap(terms[:, at * oc : (at + 1) * oc], tap, n, lc)
+            hidden = hidden + latent_tap(term[:, at * oc : (at + 1) * oc], tap, n, lc)
     hidden = silu(hidden).astype(BF16).astype(F32)
 
     for load in loads[3]:
@@ -320,18 +330,16 @@
     def _():
         up.wait_send()
 
-    handover.wait_send()
-    if chips > 1:
-        spread.wait_send()
-    residual = latent.astype(F32)
+    for h in range(2):
+        handover(h).wait_send()
+        if chips > 1:
+            spread(h).wait_send()
     for h in range(2):
         if chips > 1:
             scatter(h).wait_recv()
-        total = jnp.sum(incoming[h].astype(F32), axis=0)
+        total = jnp.sum(incoming[h].astype(F32), axis=0) + own_latents[h].astype(F32)
         for k in range(nk):
-            whole = h * nk + k
-            piece = residual[whole // 2 * lc : (whole // 2 + 1) * lc, whole % 2 * hw : (whole % 2 + 1) * hw]
-            out[0, :, pl.ds(whole * hw, hw)] = (total[k * lc : (k + 1) * lc] + piece).astype(BF16)
+            out[0, :, pl.ds((h * nk + k) * hw, hw)] = total[k * lc : (k + 1) * lc].astype(BF16)
 
     for h in range(2):
         swap(h).wait_send()
@@ -361,11 +369,11 @@
             pltpu.VMEM(second.shape, BF16),
             pltpu.VMEM(weight_mix.shape, BF16),
             pltpu.VMEM(last.shape, BF16),
-            pltpu.VMEM((lw, lw), BF16),
+            pltpu.VMEM((2 * ch, lw // 2), BF16),
             pltpu.VMEM((gs * 16, gs * 16), BF16),
             pltpu.VMEM((gs * 16, gs * 16), BF16),
-            pltpu.VMEM((2, n // 2, 16, lw), BF16),
-            pltpu.VMEM((n * lc, cl), BF16),
+            pltpu.VMEM((2, 2, n // 2, 16, lw // 2), BF16),
+            pltpu.VMEM((2, n * lc, cl // 2), BF16),
             pltpu.VMEM((2, 2, n // 2, 16, lw // 2), BF16),
             pltpu.VMEM((2, n // 2, 16, lw // 2), BF16),
             pltpu.VMEM((2, n // 2, 16, lw // 2), BF16),
@@ -374,10 +382,10 @@
             dma,
             dma((2,)),
             dma((2,)),
-            dma,
-            dma,
-            dma,
-            dma,
+            dma((2,)),
+            dma((2,)),
+            dma((2,)),
+            dma((2,)),
             dma((2,)),
             dma((2,)),
             dma((2,)),

time: 28 us -> 27.8 us (level)
  no operation moved by 1% of the time
where the time goes in v8:
time: 27.8 us; the launch traced here: 27.6 us
  Pallas kernels  26.3 us (95%)
  local copies, waits for them, and re-layouts  1.33 us (5%)
    pallas_call x1, Pallas kernels, local(): pl.pallas_call(functools.partial(kernel, n), out_shape=jax.ShapeDtypeStru...  26.3 us
    unnamed x1, local copies, waits for them, and re-layouts  1.33 us

profile of v8, /device:TPU:0, one launch (start us, length us, event | category | flops | bytes accessed | tf_op | source)
XLA Modules:
  0.0 27.6 jit_solution(16636824801832879712)
XLA Ops:
  0.0 26.3 %shard_map.55 = bf16[1,4,2048]{2,1,0:T(4,128)(2,1)} custom-call(bf16[4,16,512]{2,1,0:T(8,128)(2,1)} %px.1, bf16[3,1536,512]{2,1,0:T(8,128)(2,1)} %bitcast.3, bf16[3,1536,512]{2,1,0:T(8,128)(2,1)} %bitcast.4, bf16[3,3,2048,128]{3,2,1,0:T(8,128)(2,1)} %wm.1, bf16[3,384,2048]{2,1,0:T(8,128)(2,1)} %bitcast.5), custom_call_target="tpu_custom_call" | custom-call | tf_op jit(solution)/shard_map/pallas_call | solution.py:361
  26.3 1.3 %copy.7 = bf16[1,4,2048]{2,1,0:T(4,128)(2,1)} copy(bf16[1,4,2048]{2,1,0:T(4,128)(2,1)} %shard_map.55) | data formatting | bytes 32768

commit v9 on v8

--- a/solution.py
+++ b/solution.py
@@ -75,7 +75,7 @@
 
 def kernel(
     n, px, w1, w2, wm, wo, out,
-    ext, w1v, w2v, wmv, wov, mix_sel, sort_sel, back_sel, gathered, latents, outgoing, swapped, paired, incoming,
+    ext, w1v, w2v, wmv, wov, mix_sel, sort_sel, back_sel, gathered, latents, outgoing, swapped, paired, incoming, result,
     wsem, psem, hsend, hrecv, gsend, grecv, fsend, frecv, xsend, xrecv, ssend, srecv,
 ):
     me = lax.axis_index("rows")
@@ -339,12 +339,15 @@
             scatter(h).wait_recv()
         total = jnp.sum(incoming[h].astype(F32), axis=0) + own_latents[h].astype(F32)
         for k in range(nk):
-            out[0, :, pl.ds((h * nk + k) * hw, hw)] = total[k * lc : (k + 1) * lc].astype(BF16)
-
+            result[0, :, pl.ds((h * nk + k) * hw, hw)] = total[k * lc : (k + 1) * lc].astype(BF16)
+
+    finish = pltpu.make_async_copy(result, out, psem)
+    finish.start()
     for h in range(2):
         swap(h).wait_send()
         if chips > 1:
             scatter(h).wait_send()
+    finish.wait()
 
 
 def local(n, pixels, weight_first, weight_second, weight_mix, weight_out):
@@ -362,7 +365,7 @@
         functools.partial(kernel, n),
         out_shape=jax.ShapeDtypeStruct((rows // 4, lc, cl), BF16),
         in_specs=[pl.BlockSpec(memory_space=pl.ANY)] * 5,
-        out_specs=pl.BlockSpec(memory_space=pltpu.VMEM),
+        out_specs=pl.BlockSpec(memory_space=pl.ANY),
         scratch_shapes=[
             pltpu.VMEM((rows + 4, cols, ch), BF16),
             pltpu.VMEM(first.shape, BF16),
@@ -378,6 +381,7 @@
             pltpu.VMEM((2, n // 2, 16, lw // 2), BF16),
             pltpu.VMEM((2, n // 2, 16, lw // 2), BF16),
             pltpu.VMEM((2, n // 2, 16, lw // 2), BF16),
+            pltpu.VMEM((rows // 4, lc, cl), BF16),
             dma((4, 3)),
             dma,
             dma((2,)),
@@ -392,7 +396,7 @@
             dma((2,)),
         ],
         compiler_params=pltpu.CompilerParams(
-            collective_id=0, has_side_effects=True, vmem_limit_bytes=56 * 1024 * 1024
+            collective_id=0, has_side_effects=True, vmem_limit_bytes=55168 * 1024
         ),
     )(pixels, first, second, weight_mix, last)
 

time: 27.8 us -> 26.4 us (0.950)
  local copies, waits for them, and re-layouts: 1.33 us -> 0.61 us
  Pallas kernels: 26.3 us -> 25.7 us
    unnamed x1, local copies, waits for them, and re-layouts: 1.33 us -> 0.61 us
    pallas_call x1, Pallas kernels: 26.3 us -> 25.7 us  [local(): pl.pallas_call(functools.partial(kernel, n), out_shape=jax.ShapeDtypeStru...]
where the time goes in v9:
time: 26.4 us; the launch traced here: 26.3 us
  Pallas kernels  25.7 us (97%)
  local copies, waits for them, and re-layouts  0.61 us (2%)
    pallas_call x1, Pallas kernels, local(): pl.pallas_call(functools.partial(kernel, n), out_shape=jax.ShapeDtypeStru...  25.7 us
    unnamed x1, local copies, waits for them, and re-layouts  0.61 us

profile of v9, /device:TPU:0, one launch (start us, length us, event | category | flops | bytes accessed | tf_op | source)
XLA Modules:
  0.0 26.3 jit_solution(2556031867464073638)
XLA Ops:
  0.0 25.7 %shard_map.55 = bf16[1,4,2048]{2,1,0:T(4,128)(2,1)S(1)} custom-call(bf16[4,16,512]{2,1,0:T(8,128)(2,1)} %px.1, bf16[3,1536,512]{2,1,0:T(8,128)(2,1)} %bitcast.3, bf16[3,1536,512]{2,1,0:T(8,128)(2,1)} %bitcast.4, bf16[3,3,2048,128]{3,2,1,0:T(8,128)(2,1)} %wm.1, bf16[3,384,2048]{2,1,0:T(8,128)(2,1)} %bitcast.5), custom_call_target="tpu_custom_call" | custom-call | tf_op jit(solution)/shard_map/pallas_call | solution.py:364
  25.7 0.6 %copy.7 = bf16[1,4,2048]{2,1,0:T(4,128)(2,1)} copy(bf16[1,4,2048]{2,1,0:T(4,128)(2,1)S(1)} %shard_map.55) | data formatting | bytes 32768

commit v10 on v9

--- a/solution.py
+++ b/solution.py
@@ -296,7 +296,11 @@
         )
 
     def multiply(h):
-        parts = [contribution((h * nk + k) * hw) for k in range(nk)]
+        parts = []
+        for k in range(nk):
+            if h == 1 and k == nk - 1:
+                send_sums(0)
+            parts.append(contribution((h * nk + k) * hw))
         for g in range(n // gs):
             block = jnp.concatenate([part[g * span : (g + 1) * span] for part in parts], axis=0)
             block = dot(back_sel[...], block).astype(BF16).reshape(2, gs // 2, 16, hw)
@@ -319,7 +323,6 @@
 
     multiply(0)
     multiply(1)
-    send_sums(0)
     send_sums(1)
 
     @pl.when(me < n - 1)

time: 26.4 us -> 26.9 us (1.019)
  Pallas kernels: 25.7 us -> 26.1 us
    pallas_call x1, Pallas kernels: 25.7 us -> 26.1 us  [local(): pl.pallas_call(functools.partial(kernel, n), out_shape=jax.ShapeDtypeStru...]
where the time goes in v10:
time: 26.9 us; the launch traced here: 26.7 us
  Pallas kernels  26.1 us (97%)
  local copies, waits for them, and re-layouts  0.61 us (2%)
    pallas_call x1, Pallas kernels, local(): pl.pallas_call(functools.partial(kernel, n), out_shape=jax.ShapeDtypeStru...  26.1 us
    unnamed x1, local copies, waits for them, and re-layouts  0.61 us

profile of v10, /device:TPU:0, one launch (start us, length us, event | category | flops | bytes accessed | tf_op | source)
XLA Modules:
  0.0 26.7 jit_solution(1931248547661445136)
XLA Ops:
  0.0 26.1 %shard_map.55 = bf16[1,4,2048]{2,1,0:T(4,128)(2,1)S(1)} custom-call(bf16[4,16,512]{2,1,0:T(8,128)(2,1)} %px.1, bf16[3,1536,512]{2,1,0:T(8,128)(2,1)} %bitcast.3, bf16[3,1536,512]{2,1,0:T(8,128)(2,1)} %bitcast.4, bf16[3,3,2048,128]{3,2,1,0:T(8,128)(2,1)} %wm.1, bf16[3,384,2048]{2,1,0:T(8,128)(2,1)} %bitcast.5), custom_call_target="tpu_custom_call" | custom-call | tf_op jit(solution)/shard_map/pallas_call | solution.py:367
  26.1 0.6 %copy.7 = bf16[1,4,2048]{2,1,0:T(4,128)(2,1)} copy(bf16[1,4,2048]{2,1,0:T(4,128)(2,1)S(1)} %shard_map.55) | data formatting | bytes 32768
